TPU v7x, 128 devices: a whole 4x4x4 slice. The times are simulated.
128 devices in a mesh: gx: 4 (over z_hi, core), yz: 32 (over z_lo, y, x).
Axes of the slice: x: 4, y: 4, z: 4 (z_hi: 2, z_lo: 2; z = z_hi * 2 + z_lo), core: 2. Of those that a mesh axis runs over, the one named last changes fastest.
Arguments:
- positions: float32 [3, 4, 32, 512], P(None, 'gx', 'yz'), may hold values from -0.35 to 0.35
- species: int32 [4, 32, 512], P('gx', 'yz'), may hold values from 0 to 7
- neighbors: int32 [4, 32, 512, 48], P('gx', 'yz'), may hold values from 0 to 4607, as said below
- slot_used: int32 [4, 32, 512, 48], P('gx', 'yz'), may hold values from 0 to 1, as said below
- embed_weight: bfloat16 [24, 128], replicated, may hold values from -1.25 to 1.25
- first_weight: bfloat16 [128, 32], replicated, may hold values from -0.5 to 0.5
- env_weight: bfloat16 [2, 128, 32], replicated, may hold values from -0.5 to 0.5
- latent_weight: bfloat16 [2, 224, 128], replicated, may hold values from -0.375 to 0.375
- mix_weight: bfloat16 [1, 3, 32, 32], replicated, may hold values from -1 to 1
- out_weight: bfloat16 [128, 128], replicated, may hold values from -0.5 to 0.5
- out_vector: float32 [128], replicated, may hold values from -0.5 to 0.5
Outputs:
- atom_energy: float32 [4, 32, 512], P('gx', 'yz')
- forces: float32 [3, 4, 32, 512], P(None, 'gx', 'yz')
Inputs may be any that keep to these rules, and one draw needn't show every extreme that they name: `neighbors`: entry (g, y, k, s) names the neighbour in slot s of site k of the device at (g, y), as in the first step. A site's neighbours are distinct lattice points other than its own, at most 2 steps from it along each of x, y and z. `slot_used`: atoms fill each device's sites from site 0 upward. In every row of devices along yz (one gx index), a quarter of the devices hold atoms at all 512 sites and the others at 64 to 128 sites, some exactly 128. A slot is used exactly where its site and the named neighbour site both hold atoms.
All inputs are finite; a program needn't handle non-finite values.
Results may differ from a plain program's by a relative error of at most 0.017.
Values sent between devices are 32-bit elements; how exact they have to be, the bound alone decides.
No kernel may reach another device: no remote copies, remote signals or barrier semaphores. Data moves between devices by JAX's collectives and lax.ppermute only.
A program may use at most 128 MiB of HBM per device.

v0:
```python
import math

import jax
import jax.numpy as jnp
import numpy as np
from jax import lax
from jax.sharding import PartitionSpec as P

LX = 8
LY = 8
LZ = 8
NRAD = 8
NSPEC = 8


CUTOFF = 5.0
DEGREE_MAP = np.array([0, 1, 1, 1, 2, 2, 2, 2, 2])


def shifted(shard, axis, by):
    count = lax.axis_size(axis)
    return lax.ppermute(shard, axis, [(i, (i + by) % count) for i in range(count)])


def extended(block, sides, width):
    for axis, dim in sides:
        count = lax.axis_size(axis)
        forward = [(i, i + 1) for i in range(count - 1)]
        forward.append((count - 1, 0))
        backward = [(target, source) for source, target in forward]
        low = lax.ppermute(
            lax.slice_in_dim(block, block.shape[dim] - width, None, axis=dim), axis, forward
        )
        high = lax.ppermute(lax.slice_in_dim(block, 0, width, axis=dim), axis, backward)
        block = jnp.concatenate([low, block, high], axis=dim)
    return block


def lattice(site_index):
    return (site_index // (LY * LZ), site_index // LZ % LY, site_index % LZ)


def lattice_steps(centre_site, side_gx, side_yz, far_site):
    centre_x, centre_y, centre_z = lattice(centre_site)
    far_x, far_y, far_z = lattice(far_site)
    step_x = (side_gx - 1) * LX + far_x - centre_x[:, None]
    step_y = (side_yz - 1) * LY + far_y - centre_y[:, None]
    step_z = (far_z - centre_z[:, None] + LZ // 2) % LZ - LZ // 2
    return jnp.stack([step_x, step_y, step_z], -1).astype(jnp.float32)


def geometry(displace, in_use):
    length = jnp.sqrt(jnp.sum(displace * displace, axis=-1))
    direct = displace / length[..., None]
    scaled = length / CUTOFF
    envelope = (1.0 - 28.0 * scaled**6 + 48.0 * scaled**7 - 21.0 * scaled**8) * in_use
    orders = jnp.arange(1, NRAD + 1).astype(jnp.float32)
    radial = (
        math.sqrt(2.0 / CUTOFF)
        * jnp.sin(orders * (math.pi / CUTOFF) * length[..., None])
        / length[..., None]
    )
    along_x, along_y, along_z = (direct[..., 0], direct[..., 1], direct[..., 2])
    root_three, root_five, root_fifteen = (math.sqrt(3.0), math.sqrt(5.0), math.sqrt(15.0))
    harmonic = jnp.stack(
        [
            jnp.ones_like(along_x),
            root_three * along_x,
            root_three * along_y,
            root_three * along_z,
            root_fifteen * along_x * along_y,
            root_fifteen * along_y * along_z,
            0.5 * root_five * (3.0 * along_z * along_z - 1.0),
            root_fifteen * along_x * along_z,
            0.5 * root_fifteen * (along_x * along_x - along_y * along_y),
        ],
        -1,
    )
    return jnp.concatenate([radial, harmonic, envelope[..., None]], -1)


def network(
    features,
    kind_centre,
    kind_far,
    embed_weight,
    first_weight,
    env_weight,
    latent_weight,
    mix_weight,
    out_weight,
    out_vector,
):
    radial = features[..., :NRAD]
    harmonic = features[..., NRAD : NRAD + 9]
    envelope = features[..., NRAD + 9 : NRAD + 10]
    catalog = jnp.arange(NSPEC).astype(jnp.float32)
    centre_hot = (kind_centre[:, None] == catalog).astype(jnp.float32)
    far_hot = (kind_far[..., None] == catalog).astype(jnp.float32)
    inputs = jnp.concatenate(
        [radial, jnp.broadcast_to(centre_hot[:, None, :], far_hot.shape), far_hot], -1
    )
    latent = (
        jax.nn.silu(
            jnp.dot(inputs.astype(jnp.bfloat16), embed_weight, preferred_element_type=jnp.float32)
        )
        * envelope
    )
    channel_weights = jnp.dot(
        latent.astype(jnp.bfloat16), first_weight, preferred_element_type=jnp.float32
    )
    tensor = channel_weights[..., None, :] * harmonic[..., :, None]
    layers = env_weight.shape[0]
    norm_scale = 1.0 / math.sqrt(features.shape[1])
    for layer_no in range(layers):
        env_coeff = jnp.dot(
            latent.astype(jnp.bfloat16), env_weight[layer_no], preferred_element_type=jnp.float32
        )
        environ = (
            jnp.sum(env_coeff[..., None, :] * harmonic[..., :, None], axis=1, keepdims=True)
            * norm_scale
        )
        scalar_zero = tensor[..., 0, :] * environ[..., 0, :]
        scalar_one = jnp.sum(tensor[..., 1:4, :] * environ[..., 1:4, :], axis=-2)
        scalar_two = jnp.sum(tensor[..., 4:9, :] * environ[..., 4:9, :], axis=-2)
        joined = jnp.concatenate([latent, scalar_zero, scalar_one, scalar_two], -1)
        latent = (
            latent
            + jax.nn.silu(
                jnp.dot(
                    joined.astype(jnp.bfloat16),
                    latent_weight[layer_no],
                    preferred_element_type=jnp.float32,
                )
            )
            * envelope
        )
        if layer_no + 1 < layers:
            product = tensor * environ[..., 0:1, :] + tensor[..., 0:1, :] * environ
            channel_mix = mix_weight[layer_no].astype(jnp.float32)[DEGREE_MAP]
            tensor = jnp.einsum(
                "cnmk,mkj->cnmj", product, channel_mix, precision=lax.Precision.HIGHEST
            )
    hidden = jax.nn.silu(
        jnp.dot(latent.astype(jnp.bfloat16), out_weight, preferred_element_type=jnp.float32)
    )
    pair_energy = jnp.sum(hidden * out_vector, axis=-1) * envelope[..., 0]
    return jnp.sum(pair_energy, axis=1)


def pair_terms(displace, in_use, kind_centre, kind_far, params):

    def energy_of(moved):
        return network(geometry(moved, in_use), kind_centre, kind_far, *params)

    energy, pull_back = jax.vjp(energy_of, displace)
    (gradient,) = pull_back(jnp.ones_like(energy))
    return (energy, gradient)


def in_groups(kernel, arrays):
    item_count = arrays[0].shape[0]
    group_size = math.gcd(item_count, 32)
    groups = item_count // group_size
    stacked = tuple((array.reshape((groups, group_size) + array.shape[1:]) for array in arrays))
    results = lax.map(lambda portion: kernel(*portion), stacked)
    return jax.tree.map(lambda result: result.reshape((item_count,) + result.shape[2:]), results)


def along_yz(partial_force, offset):
    return shifted(partial_force, "yz", offset)


def along_gx(partial_force, offset):
    return shifted(partial_force, "gx", offset)


def on_device(
    positions,
    species,
    neighbors,
    slot_used,
    embed_weight,
    first_weight,
    env_weight,
    latent_weight,
    mix_weight,
    out_weight,
    out_vector,
):
    params = (
        embed_weight,
        first_weight,
        env_weight,
        latent_weight,
        mix_weight,
        out_weight,
        out_vector,
    )
    atom_count = species.shape[-1]
    slot_count = neighbors.shape[-1]
    owned_rows = jnp.concatenate([positions, species.astype(jnp.float32)[None]], 0)
    ghosted = extended(owned_rows, (("gx", 1), ("yz", 2)), 1)
    table_all = ghosted.reshape(4, 9 * atom_count)
    listed = neighbors.reshape(atom_count, slot_count)
    picked = table_all[:, listed]
    centre_site = jnp.arange(atom_count, dtype=jnp.int32)
    side_index = listed // atom_count
    offsets = lattice_steps(centre_site, side_index // 3, side_index % 3, listed % atom_count)
    coords = positions.reshape(3, atom_count).T
    displace = jnp.moveaxis(picked[:3], 0, -1) - coords[:, None, :] + offsets
    kind_far = picked[3]
    kind_centre = species.reshape(atom_count).astype(jnp.float32)
    in_use = slot_used.reshape(atom_count, slot_count).astype(jnp.float32)
    energy, gradient = in_groups(
        lambda moved, used_slots, centre_kind, far_kind: pair_terms(
            moved, used_slots, centre_kind, far_kind, params
        ),
        (displace, in_use, kind_centre, kind_far),
    )
    centre_force = jnp.sum(gradient, axis=1).T
    pulled = jax.ops.segment_sum(
        gradient.reshape(atom_count * slot_count, 3),
        listed.reshape(-1),
        num_segments=9 * atom_count,
    )
    spread = (-pulled.T).reshape(3, 3, 3, atom_count)
    spread = spread.at[:, 1, 1, :].add(centre_force)
    column = spread[:, :, 1, :] + along_yz(spread[:, :, 0, :], -1) + along_yz(spread[:, :, 2, :], 1)
    forces = column[:, 1, :] + along_gx(column[:, 0, :], -1) + along_gx(column[:, 2, :], 1)
    return (energy.reshape(1, 1, atom_count), forces.reshape(3, 1, 1, atom_count))


def solution(mesh):
    in_specs = (
        P(None, "gx", "yz", None),
        P("gx", "yz", None),
        P("gx", "yz", None, None),
        P("gx", "yz", None, None),
        P(),
        P(),
        P(),
        P(),
        P(),
        P(),
        P(),
    )
    out_specs = (P("gx", "yz", None), P(None, "gx", "yz", None))
    return jax.shard_map(
        on_device, mesh=mesh, in_specs=in_specs, out_specs=out_specs, check_vma=False
    )
```

profile of v0, /device:TPU:1, one launch (start us, length us, event | category | flops | bytes accessed | tf_op | source)
XLA Modules:
  0.0 1248.3 jit_solution(16452971751709778976)
XLA Ops:
  2.0 5.0 collective-permute-start
  13.6 4.5 collective-permute-start.3
  24.4 81.3 %gather_fusion.1 = f32[24576,4]{1,0:T(8,128)} fusion(f32[4,4608]{0,1:T(8,128)S(1)} %bitcast.416, s32[24576]{0:T(1024)S(1)} %broadcast_clamp_fusion), kind=kCustom, calls=%fused_computation.1 | custom fusion | bytes 884736 | tf_op jit(solution)/shard_map/gather | solution.py:206
  105.8 7.7 copy.151
  115.2 973.7 %while.16 = (s32[]{:T(128)}, f32[16,32]{1,0:T(8,128)}, f32[16,32,48,3]{2,1,3,0:T(8,128)}, f32[16,32,48,3]{2,1,3,0:T(8,128)S(1)}, f32[16,32]{1,0:T(8,128)}, /*ind...) while((s32[]{:T(128)}, f32[16,32]{1,0:T(8,128)}, ...), condition=%wide.region_31.32_spmd.clone, body=%wide.region_0.31_spmd.sunk.clone.sunk | while | flops 935751936 | bytes 101266456 | solution.py:166
  147.1 6.3 fusion.286
  164.8 4.7 fusion.291
  169.5 4.2 multiply_reduce_fusion.45
  177.8 6.3 multiply_reduce_fusion.50
  206.8 6.3 fusion.286
  224.5 4.7 fusion.291
  229.3 4.2 multiply_reduce_fusion.45
  237.6 6.3 multiply_reduce_fusion.50
  266.6 6.3 fusion.286
  284.3 4.7 fusion.291
  289.0 4.2 multiply_reduce_fusion.45
  297.3 6.3 multiply_reduce_fusion.50
  326.4 6.3 fusion.286
  344.0 4.7 fusion.291
  348.8 4.2 multiply_reduce_fusion.45
  357.1 6.3 multiply_reduce_fusion.50
  386.1 6.3 fusion.286
  403.8 4.7 fusion.291
  408.6 4.2 multiply_reduce_fusion.45
  416.8 6.3 multiply_reduce_fusion.50
  445.9 6.3 fusion.286
  463.6 4.7 fusion.291
  468.3 4.2 multiply_reduce_fusion.45
  476.6 6.3 multiply_reduce_fusion.50
  505.7 6.3 fusion.286
  523.3 4.7 fusion.291
  536.4 6.3 multiply_reduce_fusion.50
  565.4 6.3 fusion.286
  583.1 4.7 fusion.291
  596.1 6.3 multiply_reduce_fusion.50
  625.2 6.3 fusion.286
  642.9 4.7 fusion.291
  655.9 6.3 multiply_reduce_fusion.50
  684.9 6.3 fusion.286
  702.6 4.7 fusion.291
  715.6 6.3 multiply_reduce_fusion.50
  744.7 6.3 fusion.286
  762.4 4.7 fusion.291
  767.1 4.2 multiply_reduce_fusion.45
  775.4 6.3 multiply_reduce_fusion.50
  804.4 6.3 fusion.286
  822.1 4.7 fusion.291
  835.2 6.3 multiply_reduce_fusion.50
  864.2 6.3 fusion.286
  881.9 4.7 fusion.291
  894.9 6.3 multiply_reduce_fusion.50
  923.9 6.3 fusion.286
  941.6 4.7 fusion.291
  954.6 6.3 multiply_reduce_fusion.50
  983.7 6.3 fusion.286
  1001.4 4.7 fusion.291
  1014.4 6.3 multiply_reduce_fusion.50
  1043.4 6.3 fusion.286
  1061.1 4.7 fusion.291
  1065.9 4.2 multiply_reduce_fusion.45
  1074.1 6.3 multiply_reduce_fusion.50
  1088.9 8.2 copy.178
  1097.5 131.5 %scatter_custom_fusion = f32[4608,3]{1,0:T(8,128)S(1)} fusion(s32[24576]{0:T(1024)} %reshape.880, f32[24576,3]{1,0:T(8,128)} %bitcast.418, f32[]{:T(128)} %constant.288.clone.1), kind=kCustom, calls=%fused_computation.279 | custom fusion | flops 73728 | bytes 55808 | tf_op jit(solution)/shard_map/scatter-add | solution.py:222
  1236.6 6.0 collective-permute-done.5
  (2187 shorter events, 662.5 us)
Async XLA Ops:
  2.0 6.6 collective-permute-start
  7.0 4.6 collective-permute-start.1
  12.3 10.7 collective-permute-start.2
  13.6 9.4 collective-permute-start.3
  105.8 9.5 copy-start.10
  105.8 9.5 copy-start.17
  105.8 9.5 copy-start.21
  105.8 9.5 copy-start.29
  132.8 7.1 copy-start.11
  132.8 7.1 copy-start.19
  137.3 7.9 copy-start.24
  144.5 8.8 slice-start
  177.8 10.7 copy-start.18
  197.1 7.9 copy-start.24
  204.3 8.8 slice-start
  237.6 10.7 copy-start.18
  256.8 7.9 copy-start.24
  264.0 8.8 slice-start
  297.3 10.7 copy-start.18
  316.6 7.9 copy-start.24
  323.8 8.8 slice-start
  357.1 10.7 copy-start.18
  376.3 7.9 copy-start.24
  383.5 8.8 slice-start
  416.8 10.7 copy-start.18
  436.1 7.9 copy-start.24
  443.3 8.8 slice-start
  476.6 10.7 copy-start.18
  495.9 7.9 copy-start.24
  503.1 8.8 slice-start
  536.4 10.7 copy-start.18
  555.6 7.8 copy-start.24
  562.8 8.8 slice-start
  596.1 10.7 copy-start.18
  615.4 7.9 copy-start.24
  622.6 8.8 slice-start
  655.9 10.7 copy-start.18
  675.1 7.9 copy-start.24
  682.3 8.8 slice-start
  715.6 10.7 copy-start.18
  734.9 7.9 copy-start.24
  742.1 8.8 slice-start
  775.4 10.7 copy-start.18
  794.6 7.9 copy-start.24
  801.9 8.8 slice-start
  835.1 10.7 copy-start.18
  854.4 7.9 copy-start.24
  861.6 8.8 slice-start
  894.9 10.7 copy-start.18
  914.1 7.9 copy-start.24
  921.3 8.8 slice-start
  954.6 10.7 copy-start.18
  973.9 7.9 copy-start.24
  981.1 8.8 slice-start
  1014.4 10.7 copy-start.18
  1033.6 7.9 copy-start.24
  1040.8 8.8 slice-start
  1074.1 10.7 copy-start.18
  1088.9 8.3 copy-start.14
  1097.2 148.9 %copy-start.26 = (f32[16,32]{1,0:T(8,128)S(1)}, f32[16,32]{1,0:T(8,128)}, u32[]{:S(2)}) copy-start(f32[16,32]{1,0:T(8,128)} %get-tuple-element.653) | copy-start | bytes 6148
  1233.6 3.0 collective-permute-start.4
  1235.7 6.9 collective-permute-start.5
  1242.6 4.7 collective-permute-start.6
  1242.8 4.5 collective-permute-start.7
  (414 other events, 1655.5 us)
where the time goes:
time: 1260 us; the launch traced here: 1250 us
  other arithmetic  624 us (50%)
  matrix products  317 us (25%)
  local copies, waits for them, and re-layouts  249 us (20%)
  loops' own time  30.1 us (2%)
  starting transfers between devices  16.2 us (1%)
    dot_general x32, matrix products, network(): jnp.einsum('cnmk,mkj->cnmj', product, channel_mix, precision=lax.Precisio...  176 us
    reduce_sum x32, other arithmetic, network(): env_coeff[..., None, :] * harmonic[..., :, None]  135 us
    scatter-add x1, other arithmetic, on_device(): jax.ops.segment_sum(gradient.reshape(atom_count * slot_count, 3), listed....  131 us
    reduce_sum x16, other arithmetic, network(): tensor = channel_weights[..., None, :] * harmonic[..., :, None]  101 us
    gather x2, local copies, waits for them, and re-layouts, on_device(): picked = table_all[:, listed]  89 us
    while x944, local copies, waits for them, and re-layouts  59.5 us
    dot_general x64, matrix products, network(): jnp.dot(latent.astype(jnp.bfloat16), env_weight[layer_no], preferred_elem...  40.7 us
    reduce_sum x48, other arithmetic, network(): scalar_two = jnp.sum(tensor[..., 4:9, :] * environ[..., 4:9, :], axis=-2)  39.6 us
  transfers between devices with their start and end apart: 8, of which 4 were waited for; matrix products, arithmetic and copies ran while one was open for 1% of the time, Pallas kernels for 0%

commit v1 on v0

v1 whole, which is shorter than its diff:
```python
import functools
import math

import jax
import jax.numpy as jnp
import numpy as np
from jax import lax
from jax.experimental import pallas as pl
from jax.experimental.pallas import tpu as pltpu
from jax.sharding import PartitionSpec as P

F32 = jnp.float32
BF16 = jnp.bfloat16
LZ = 8
NRAD = 8
CH = 32
SLOTS = 48
GROUP = 16
PAIRS = GROUP * SLOTS
UNIT = 2
CHUNK = 8
TILE = 256
NORM = 1.0 / math.sqrt(SLOTS)
RADIAL_GAIN = math.sqrt(2.0 / 5.0)
DEGREES = ((0,), (1, 2, 3), (4, 5, 6, 7, 8))
ORDER = (1, 2, 3, 4, 5, 6, 7, 8, 0)
DEGREE_OF = tuple(next(d for d in range(3) if m in DEGREES[d]) for m in ORDER)


def nn(a, b):
    return jnp.dot(a, b, preferred_element_type=F32)


def nt(a, b):
    return lax.dot_general(a, b, (((1,), (1,)), ((), ())), preferred_element_type=F32)


def tn(a, b):
    return lax.dot_general(a, b, (((0,), (0,)), ((), ())), preferred_element_type=F32)


def pieces(value, count):
    out = []
    for _ in range(count):
        part = value.astype(BF16).astype(F32)
        out.append(part)
        value = value - part
    return out


def constants():
    lane = np.arange(PAIRS)
    atom_mask = (lane[None, :] // SLOTS == np.arange(GROUP)[:, None]).astype(np.float32)
    slot_pick = (lane[None, :] % SLOTS == np.arange(SLOTS)[:, None]).astype(np.float32)
    wide = np.arange(GROUP * CH)
    atom_wide = (wide[None, :] // CH == np.arange(GROUP)[:, None]).astype(np.float32)
    chan_wide = (wide[None, :] % CH == np.arange(CH)[:, None]).astype(np.float32)
    degree_mask = np.zeros((96, 144), np.float32)
    for i, d in enumerate(DEGREE_OF):
        degree_mask[d * 32 : d * 32 + 32, i * 16 : i * 16 + 16] = 1.0
    return atom_mask, slot_pick, atom_wide, chan_wide, degree_mask


def geometry(get, put, geo):
    used = get(14) > 0.5
    one = jnp.ones((CHUNK, PAIRS), F32)
    nil = jnp.zeros((CHUNK, PAIRS), F32)
    vx = jnp.where(used, get(0) + (get(3) + get(6)) + get(9), one)
    vy = jnp.where(used, get(1) + (get(4) + get(7)) + get(10), nil)
    step_z = get(11)
    step_z = jnp.where(step_z >= 4.0, step_z - 8.0, jnp.where(step_z < -4.0, step_z + 8.0, step_z))
    vz = jnp.where(used, get(2) + (get(5) + get(8)) + step_z, nil)
    keep = jnp.where(used, one, nil)
    square = vx * vx + vy * vy + vz * vz
    inv = lax.rsqrt(square)
    inv = inv * (1.5 - 0.5 * square * inv * inv)
    length = square * inv
    ux, uy, uz = vx * inv, vy * inv, vz * inv
    t = length * 0.2
    t2 = t * t
    t5 = t2 * t2 * t
    t6 = t5 * t
    envelope = (1.0 - 28.0 * t6 + 48.0 * t6 * t - 21.0 * t6 * t2) * keep
    slope = t5 * (-168.0 + 336.0 * t - 168.0 * t2) * (0.2 * keep)
    y = length * (math.pi / 5.0) - (math.pi / 2.0)
    y2 = y * y
    sine = 1.0 + y2 * (
        -1.0 / 2
        + y2 * (1.0 / 24 + y2 * (-1.0 / 720 + y2 * (1.0 / 40320 + y2 * (-1.0 / 3628800 + y2 * (1.0 / 479001600)))))
    )
    cosine = -y * (
        1.0
        + y2
        * (-1.0 / 6 + y2 * (1.0 / 120 + y2 * (-1.0 / 5040 + y2 * (1.0 / 362880 + y2 * (-1.0 / 39916800)))))
    )
    twice = 2.0 * cosine
    sines, cosines = [nil, sine], [one, cosine]
    for _ in range(NRAD - 1):
        sines.append(twice * sines[-1] - sines[-2])
        cosines.append(twice * cosines[-1] - cosines[-2])
    scale = RADIAL_GAIN * inv
    for n in range(1, NRAD + 1):
        radial = scale * sines[n]
        put(n - 1, radial)
        geo[n - 1] = ((n * math.pi / 5.0) * scale) * cosines[n] - radial * inv
    r3, r5, r15 = math.sqrt(3.0), math.sqrt(5.0), math.sqrt(15.0)
    harmonic = [
        r3 * ux,
        r3 * uy,
        r3 * uz,
        r15 * ux * uy,
        r15 * uy * uz,
        0.5 * r5 * (3.0 * uz * uz - 1.0),
        r15 * ux * uz,
        0.5 * r15 * (ux * ux - uy * uy),
    ]
    for i, value in enumerate(harmonic):
        put(8 + i, value)
    put(16, envelope)
    put(17, get(13))
    put(18, get(12))
    geo[8] = slope
    geo[9] = ux
    geo[10] = uy
    geo[11] = uz
    geo[12] = inv
    geo[13] = keep


def geometry_back(get, put, geo):
    slope, ux, uy, uz, inv, keep = (geo[8 + i] for i in range(6))
    along = get(16) * slope
    for n in range(NRAD):
        along = along + get(n) * geo[n]
    g1, g2, g3, g4, g5, g6, g7, g8 = (get(8 + i) for i in range(8))
    r3, r5, r15 = math.sqrt(3.0), math.sqrt(5.0), math.sqrt(15.0)
    ax = r3 * g1 + r15 * (uy * g4 + uz * g7 + ux * g8)
    ay = r3 * g2 + r15 * (ux * g4 + uz * g5 - uy * g8)
    az = r3 * g3 + r15 * (uy * g5 + ux * g7) + (3.0 * r5) * uz * g6
    radial_part = along - (ax * ux + ay * uy + az * uz) * inv
    for i, (a, u) in enumerate(((ax, ux), (ay, uy), (az, uz))):
        high, low = pieces(jnp.where(keep > 0.5, radial_part * u + a * inv, 0.0), 2)
        put(i, high)
        put(3 + i, low)


def swish(half):
    wide = 1.0 + jnp.tanh(half)
    value = half * wide
    return value, wide + value * (2.0 - wide)


def together(streams):
    while streams:
        left = []
        for stream in streams:
            try:
                next(stream)
                left.append(stream)
            except StopIteration:
                pass
        streams = left


def pair_kernel(
    blocks_ref,
    mid_ref,
    low_ref,
    high_ref,
    neighbors_ref,
    used_ref,
    embed_ref,
    first_ref,
    env_ref,
    latent_ref,
    mix_ref,
    out_ref,
    vector_ref,
    atom_mask_ref,
    slot_pick_ref,
    atom_wide_ref,
    chan_wide_ref,
    degree_mask_ref,
    energy_ref,
    fmid_ref,
    flow_ref,
    fhigh_ref,
    far_tab,
    own_tab,
    ftab,
    embed_t,
    we_t,
    l1_t,
    l2_t,
    e1_t,
    out_t,
    mix_t,
    mix_all,
    mix_wide,
    we_all,
    env1,
    vec_b,
    hot,
    gat,
    feat,
    dfeat,
    geo,
    x0,
    hbd,
    lat,
    dd,
    ss,
    j0,
    j1,
    w_s,
    cat,
    q_s,
    q1_s,
    a_s,
    r_s,
    ds_b,
    dl,
    t_s,
    small,
    dwr,
    e0x,
    e1x,
    bmat,
    eb,
    e0t,
    e1r,
    ww,
    pair_energy,
    db,
    outer,
    de_b,
    left,
):
    def turned(value):
        return value.astype(F32).T

    for ref in (embed_t, l1_t, l2_t, mix_t, mix_all, we_all, env1, eb, e0t, e1r, de_b):
        ref[...] = jnp.zeros_like(ref)
    embed_t[:, 0:24] = (turned(embed_ref[...]) * 0.5).astype(BF16)
    we_t[0:32, :] = turned(first_ref[...]).astype(BF16)
    we_t[32:64, :] = turned(env_ref[0]).astype(BF16)
    e1_t[...] = turned(env_ref[1]).astype(BF16)
    l1_t[:, 0:224] = (turned(latent_ref[0]) * 0.5).astype(BF16)
    l2_t[:, 0:224] = (turned(latent_ref[1]) * 0.5).astype(BF16)
    out_t[...] = (turned(out_ref[...]) * 0.5).astype(BF16)
    we_all[:, 0:64] = jnp.concatenate([first_ref[...], env_ref[0]], axis=1)
    env1[:, 0:32] = env_ref[1]
    mix_all[:, 0:96] = jnp.concatenate([mix_ref[d] for d in range(3)], axis=1)
    for d in range(3):
        mix_t[32 * d : 32 * d + 32, 0:32] = turned(mix_ref[d]).astype(BF16)
    mix_wide[...] = nn(mix_t[:, 0:32], chan_wide_ref[...])
    vec_b[...] = jnp.broadcast_to(vector_ref[...].T, (128, TILE))

    def enter(values_ref, per_plane, first_y):
        count = values_ref.shape[1]
        lane = lax.broadcasted_iota(jnp.int32, (1, count), 1)
        plane = lane // per_plane
        rest = lane - plane * per_plane
        column = rest // LZ
        lattice = [plane.astype(F32), (column + first_y).astype(F32), (rest - column * LZ).astype(F32)]
        xyz = values_ref[0:3, :]
        kind = values_ref[3:4, :]
        one = jnp.ones((1, count), F32)
        nil = jnp.zeros((1, count), F32)
        places = jnp.concatenate(pieces(xyz, 3) + lattice, axis=0)
        far = jnp.concatenate([places, kind, nil, one, nil], axis=0).T.astype(BF16)
        own = jnp.concatenate([-places, nil, kind, nil, nil], axis=0).T.astype(BF16)
        for p in range(12):
            start = p * 96 + first_y * LZ
            far_tab[start : start + per_plane, :] = far[p * per_plane : (p + 1) * per_plane, :]
            own_tab[start : start + per_plane, :] = own[p * per_plane : (p + 1) * per_plane, :]

    enter(mid_ref, 64, 2)
    enter(low_ref, 16, 0)
    enter(high_ref, 16, 10)
    ftab[...] = jnp.zeros_like(ftab)
    energy_ref[...] = jnp.zeros_like(energy_ref)
    gat[...] = jnp.zeros_like(gat)
    dfeat[...] = jnp.zeros_like(dfeat)
    hot_rows = lax.broadcasted_iota(jnp.int32, (240, PAIRS), 0).astype(F32)
    tiles = [slice(TILE * j, TILE * j + TILE) for j in range(PAIRS // TILE)]
    halves = [slice(0, 384), slice(384, 768)]
    wides = [slice(0, 256), slice(256, 512)]

    def row_base(block):
        return (block // 4) * 96 + (block % 4) * 16

    def fetch(block, slot):
        x = block // 4
        yb = block % 4
        rows = pl.ds(pl.multiple_of(block * GROUP, GROUP), GROUP)
        name = neighbors_ref[rows, :]
        side = name >> 9
        site = name & 511
        a = (side * 11) >> 5
        c = side - 3 * a
        ex = a * 8 + (site >> 6) - 6 - x
        ey = c * 8 + ((site >> 3) & 7) - 6 - 2 * yb
        local = ex * 48 + ey * 8 + (site & 7)
        local = jnp.where(used_ref[rows, :] > 0, local, -1)
        spread = nn(local.astype(F32).astype(BF16), slot_pick_ref[...])
        index = jnp.sum(spread * atom_mask_ref[...].astype(F32), axis=0, keepdims=True)
        hot[slot, 0:240, :] = jnp.where(hot_rows == index, 1.0, 0.0).astype(BF16)
        hot[slot, 240:256, :] = atom_mask_ref[...]
        base = row_base(block)
        parts = [far_tab[pl.ds(pl.multiple_of(base + 96 * i, 16), 48), :] for i in range(5)]
        parts.append(own_tab[pl.ds(pl.multiple_of(base + 208, 16), 16), :])
        table = jnp.concatenate(parts, axis=0)
        gat[slot] = tn(table, hot[slot])

    def network(block, slot):
        mask = atom_mask_ref[...].astype(F32)
        wide_mask = atom_wide_ref[...].astype(F32)

        def prepare(k):
            species_row = lax.broadcasted_iota(jnp.int32, (8, PAIRS), 0).astype(F32)
            hot_own = jnp.where(species_row == feat[slot + k, 17:18, :], 1.0, 0.0)
            hot_far = jnp.where(species_row == feat[slot + k, 18:19, :], 1.0, 0.0)
            nil = jnp.zeros((8, PAIRS), F32)
            x0[k] = jnp.concatenate([feat[slot + k, 0:8, :], hot_own, hot_far, nil], axis=0).astype(BF16)
            for i in range(8):
                hbd[k, 16 * i : 16 * i + 16, :] = (feat[slot + k, 8 + i : 9 + i, :] * mask).astype(BF16)
            hbd[k, 128:144, :] = atom_mask_ref[...]
            yield

        def env(k, cols):
            return feat[slot + k, 16:17, cols]

        sums = {}

        def gather_sum(key, part):
            sums[key] = sums[key] + part if key in sums else part

        def stage_a(k, cols):
            half = nn(embed_t[:, 0:32], x0[k, :, cols])
            yield
            value, slope = swish(half)
            ss[k, 0, :, cols] = value
            dd[k, 0, :, cols] = slope * (0.5 * env(k, cols))
            latent = value * env(k, cols)
            lat[k, 0, :, cols] = latent
            packed = latent.astype(BF16)
            j0[k, 0:128, cols] = packed
            we = nn(we_t[...], packed)
            yield
            w_s[k, :, cols] = we[0:32]
            coeff = we[32:64].astype(BF16)
            cat[k, 224:256, cols] = coeff
            gather_sum(("e0", k), nt(coeff, hbd[k, :, cols]))
            yield

        def between_a(k):
            environ = sums["e0", k] * NORM
            sums["e0", k] = environ
            eb[k, 0, :, 0:144] = (jnp.concatenate([environ] * 3, axis=0) * degree_mask_ref[...]).astype(BF16)
            e0t[k, :, 0:32] = environ.T.astype(BF16)
            yield
            spread = nn(e0t[k, :, 0:32], chan_wide_ref[...])
            yield
            for i in range(9):
                e0x[k, i : i + 1, :] = jnp.sum(
                    spread[16 * i : 16 * i + 16, :] * wide_mask, axis=0, keepdims=True
                )

        def stage_b(k, cols):
            q = nn(eb[k, 0, :, 0:144], hbd[k, :, cols])
            yield
            q_s[k, :, cols] = q
            w3 = jnp.concatenate([w_s[k, :, cols]] * 3, axis=0)
            scal = (q * w3).astype(BF16)
            j0[k, 128:224, cols] = scal
            half = nn(l1_t[:, 0:224], j0[k, :, cols])
            mixed = nn(mix_t[:, 0:32], scal[0:32])
            yield
            a_s[k, :, cols] = mixed
            value, slope = swish(half)
            ss[k, 1, :, cols] = value
            dd[k, 1, :, cols] = slope * (0.5 * env(k, cols))
            latent = lat[k, 0, :, cols] + value * env(k, cols)
            lat[k, 1, :, cols] = latent
            packed = latent.astype(BF16)
            j1[k, 0:128, cols] = packed
            coeff = nn(e1_t[...], packed)
            yield
            coeff = coeff.astype(BF16)
            cat[k, 192:224, cols] = coeff
            gather_sum(("e1", k), nt(coeff, hbd[k, :, cols]))
            yield

        def spread_w(k, half):
            w = w_s[k, :, halves[half]]
            m8 = mask[8 * half : 8 * half + 8, halves[half]]
            return jnp.concatenate([w * m8[p : p + 1, :] for p in range(8)], axis=0).astype(BF16)

        def stage_c(k):
            environ = sums["e1", k] * NORM
            sums["e1", k] = environ
            eb[k, 1, :, 0:144] = (jnp.concatenate([environ] * 3, axis=0) * degree_mask_ref[...]).astype(BF16)
            e1r[k, :, 0:16] = jnp.concatenate(
                [environ[:, 16 * i : 16 * i + 16] for i in range(9)], axis=0
            ).astype(BF16)
            yield
            for i in range(9):
                e1x[k, 32 * i : 32 * i + 32, :] = nn(e1r[k, 32 * i : 32 * i + 32, 0:16], atom_wide_ref[...])
            for half in range(2):
                ww[k, half] = spread_w(k, half)
            yield
            for d in range(3):
                total = None
                for i in range(9):
                    if DEGREE_OF[i] == d:
                        part = e1x[k, 32 * i : 32 * i + 32, :] * e0x[k, i : i + 1, :]
                        total = part if total is None else total + part
                rows = slice(32 * d, 32 * d + 32)
                bmat[k, rows, :] = (total * mix_wide[rows, :]).astype(BF16)
            yield
            for half in range(2):
                r_s[k, :, halves[half]] = nn(bmat[k, :, wides[half]], ww[k, half])
            yield

        def stage_d(k, cols):
            q = nn(eb[k, 1, :, 0:144], hbd[k, :, cols])
            yield
            a = a_s[k, :, cols]
            q1_s[k, :, cols] = q
            j1[k, 128:224, cols] = (a * q + r_s[k, :, cols]).astype(BF16)
            half = nn(l2_t[:, 0:224], j1[k, :, cols])
            yield
            value, slope = swish(half)
            ss[k, 2, :, cols] = value
            dd[k, 2, :, cols] = slope * (0.5 * env(k, cols))
            latent = lat[k, 1, :, cols] + value * env(k, cols)
            half = nn(out_t[...], latent.astype(BF16))
            yield
            hidden, slope = swish(half)
            weighted = hidden * vec_b[...]
            t_s[k, :, cols] = weighted
            dz3 = (slope * vec_b[...] * (0.5 * env(k, cols))).astype(BF16)
            dl2 = nn(out_ref[...], dz3)
            pair_energy[k, :, cols] = jnp.sum(weighted, axis=0, keepdims=True) * env(k, cols)
            yield
            t_s[k, :, cols] = t_s[k, :, cols] + dl2 * ss[k, 2, :, cols]
            dl[k, :, cols] = dl2
            dj = nn(latent_ref[1], (dl2 * dd[k, 2, :, cols]).astype(BF16))
            yield
            dl[k, :, cols] = dl[k, :, cols] + dj[0:128]
            dscal = dj[128:224]
            ds_b[k, :, cols] = dscal.astype(BF16)
            dmix = nn(mix_all[:, 0:96], (dscal * q1_s[k, :, cols]).astype(BF16))
            dq = (dscal * a_s[k, :, cols]).astype(BF16)
            cat[k, 0:96, cols] = dq
            gather_sum(("d1", k), nt(dq, hbd[k, :, cols]))
            yield
            small[k, :, cols] = dmix

        def stage_e(k):
            row = pair_energy[k]
            high, middle, low = pieces(row, 3)
            fill = jnp.zeros((5, PAIRS), F32)
            total = nt(jnp.concatenate([high, middle, low, fill], axis=0).astype(BF16), atom_mask_ref[...])
            energy_ref[pl.ds(block + k, 1), :] = total[0:1] + (total[1:2] + total[2:3])
            for half in range(2):
                db[k, :, wides[half]] = nt(ds_b[k, :, halves[half]], ww[k, half])
                back = tn(bmat[k, :, wides[half]], ds_b[k, :, halves[half]])
                m8 = mask[8 * half : 8 * half + 8, halves[half]]
                total = back[0:32] * m8[0:1]
                for p in range(1, 8):
                    total = total + back[32 * p : 32 * p + 32] * m8[p : p + 1]
                dwr[k, :, halves[half]] = total
            yield
            inner = []
            for i in range(9):
                rows = slice(32 * DEGREE_OF[i], 32 * DEGREE_OF[i] + 32)
                piece = db[k, rows, :] * mix_wide[rows, :]
                outer[k, 32 * i : 32 * i + 32, :] = (piece * e0x[k, i : i + 1, :]).astype(BF16)
                inner.append(jnp.sum(piece * e1x[k, 32 * i : 32 * i + 32, :], axis=0, keepdims=True))
            yield
            side = nt(outer[k], atom_wide_ref[...])
            de0t = nt(jnp.concatenate([r * wide_mask for r in inner], axis=0).astype(BF16), chan_wide_ref[...])
            yield
            de = sums["d1", k] * degree_mask_ref[...]
            de = de[0:32] + de[32:64] + de[64:96]
            de = de + jnp.concatenate([side[32 * i : 32 * i + 32, :] for i in range(9)], axis=1)
            de = de * NORM
            sums["d1", k] = de
            de_b[k, 1, :, 0:144] = de.astype(BF16)
            sums["side0", k] = de0t.T

        def stage_f(k, cols):
            dcoeff = nn(de_b[k, 1, :, 0:144], hbd[k, :, cols])
            yield
            more = nn(env1[:, 0:32], dcoeff.astype(BF16))
            yield
            dl1 = dl[k, :, cols] + more
            t_s[k, :, cols] = t_s[k, :, cols] + dl1 * ss[k, 1, :, cols]
            dl[k, :, cols] = dl1
            dj = nn(latent_ref[0], (dl1 * dd[k, 1, :, cols]).astype(BF16))
            yield
            dl[k, :, cols] = dl[k, :, cols] + dj[0:128]
            dscal = [dj[128:160] + small[k, :, cols], dj[160:192], dj[192:224]]
            w = w_s[k, :, cols]
            dw = dwr[k, :, cols]
            for d in range(3):
                cat[k, 96 + 32 * d : 128 + 32 * d, cols] = (dscal[d] * w).astype(BF16)
                dw = dw + dscal[d] * q_s[k, 32 * d : 32 * d + 32, cols]
            dwr[k, :, cols] = dw
            gather_sum(("d0", k), nt(cat[k, 96:192, cols], hbd[k, :, cols]))
            yield

        def between_f(k):
            de = sums["d0", k] * degree_mask_ref[...]
            de = (de[0:32] + de[32:64] + de[64:96] + sums["side0", k]) * NORM
            de_b[k, 0, :, 0:144] = de.astype(BF16)
            yield
            e0, e1, d1 = sums["e0", k], sums["e1", k], sums["d1", k]
            tall = []
            for e in (e1, e0):
                three = jnp.concatenate([e[:, 0:128]] * 3, axis=0)
                tall.append(three * degree_mask_ref[:, 0:128])
            tall += [d1[:, 0:128], de[:, 0:128]]
            left[k] = jnp.concatenate(tall, axis=0).T.astype(BF16)
            yield

        def stage_h(k, cols):
            dcoeff = nn(de_b[k, 0, :, 0:144], hbd[k, :, cols])
            dhbd = nn(left[k], cat[k, :, cols])
            yield
            both = jnp.concatenate([dwr[k, :, cols], dcoeff], axis=0).astype(BF16)
            more = nn(we_all[:, 0:64], both)
            for i in range(8):
                dfeat[slot + k, 8 + i : 9 + i, cols] = jnp.sum(
                    dhbd[16 * i : 16 * i + 16, :] * mask[:, cols], axis=0, keepdims=True
                )
            yield
            so_far = dl[k, :, cols]
            dl0 = jnp.where(jnp.abs(so_far) < 1e30, so_far, 0.0) + more
            dz = (dl0 * dd[k, 0, :, cols]).astype(BF16)
            dradial = nn(embed_ref[...], dz)
            dfeat[slot + k, 16:17, cols] = jnp.sum(
                t_s[k, :, cols] + dl0 * ss[k, 0, :, cols], axis=0, keepdims=True
            )
            yield
            dfeat[slot + k, 0:8, cols] = dradial[0:8]

        members = range(UNIT)
        for stage, tiled in (
            (prepare, False),
            (stage_a, True),
            (between_a, False),
            (stage_b, True),
            (stage_c, False),
            (stage_d, True),
            (stage_e, False),
            (stage_f, True),
            (between_f, False),
            (stage_h, True),
        ):
            if tiled:
                together([stage(k, cols) for k in members for cols in tiles])
            else:
                together([stage(k) for k in members])

    def scatter(block, slot):
        pulled = nt(hot[slot], dfeat[slot, 0:16, :].astype(BF16))
        base = row_base(block)
        for i in range(5):
            rows = pl.ds(pl.multiple_of(base + 96 * i, 16), 48)
            ftab[rows, :] = ftab[rows, :] - pulled[48 * i : 48 * i + 48, :]
        rows = pl.ds(pl.multiple_of(base + 208, 16), 16)
        ftab[rows, :] = ftab[rows, :] + pulled[240:256, :]

    blocks = ((blocks_ref[0] + UNIT - 1) // UNIT) * UNIT

    def chunk_step(chunk, carry):
        first = chunk * CHUNK
        count = jnp.minimum(CHUNK, blocks - first)

        def rows_of(ref):
            return lambda f: jnp.concatenate([ref[b, f : f + 1, :] for b in range(CHUNK)], axis=0)

        def rows_to(ref):
            def put(f, value):
                for b in range(CHUNK):
                    ref[b, f : f + 1, :] = value[b : b + 1, :]

            return put

        def each(step, size=1):
            def turn(i, c):
                step(first + i * size, i * size)
                return c

            lax.fori_loop(0, (count + size - 1) // size, turn, 0)

        each(fetch)
        geometry(rows_of(gat), rows_to(feat), geo)
        each(network, UNIT)
        geometry_back(rows_of(dfeat), rows_to(dfeat), geo)
        each(scatter)
        return carry

    lax.fori_loop(0, (blocks + CHUNK - 1) // CHUNK, chunk_step, 0)

    def leave(force_ref, per_plane, first_y):
        rows = jnp.concatenate(
            [ftab[p * 96 + first_y * LZ : p * 96 + first_y * LZ + per_plane, :] for p in range(12)], axis=0
        )
        turned_rows = rows.T
        force_ref[...] = turned_rows[0:3] + turned_rows[3:6]

    leave(fmid_ref, 64, 2)
    leave(flow_ref, 16, 0)
    leave(fhigh_ref, 16, 10)


def pair_call(blocks, mid, low, high, neighbors, used, params):
    embed, first, env, latent, mix, out, vector = params
    sites = neighbors.shape[0]
    atom_mask, slot_pick, atom_wide, chan_wide, degree_mask = constants()
    consts = [
        jnp.asarray(atom_mask, BF16),
        jnp.asarray(slot_pick, BF16),
        jnp.asarray(atom_wide, BF16),
        jnp.asarray(chan_wide, BF16),
        jnp.asarray(degree_mask, F32),
    ]
    vm = pl.BlockSpec(memory_space=pltpu.VMEM)
    sm = pl.BlockSpec(memory_space=pltpu.SMEM)
    scratch = [
        ((1152, 16), BF16),
        ((1152, 16), BF16),
        ((1152, 16), F32),
        ((128, 128), BF16),
        ((64, 128), BF16),
        ((128, 256), BF16),
        ((128, 256), BF16),
        ((32, 128), BF16),
        ((128, 128), BF16),
        ((96, 128), BF16),
        ((32, 128), BF16),
        ((96, 512), F32),
        ((128, 128), BF16),
        ((128, 128), BF16),
        ((128, TILE), F32),
        ((CHUNK, 256, PAIRS), BF16),
        ((CHUNK, 16, PAIRS), F32),
        ((CHUNK, 24, PAIRS), F32),
        ((CHUNK, 24, PAIRS), F32),
        ((14, CHUNK, PAIRS), F32),
        ((UNIT, 32, PAIRS), BF16),
        ((UNIT, 144, PAIRS), BF16),
        ((UNIT, 2, 128, PAIRS), F32),
        ((UNIT, 3, 128, PAIRS), F32),
        ((UNIT, 3, 128, PAIRS), F32),
        ((UNIT, 224, PAIRS), BF16),
        ((UNIT, 224, PAIRS), BF16),
        ((UNIT, 32, PAIRS), F32),
        ((UNIT, 256, PAIRS), BF16),
        ((UNIT, 96, PAIRS), F32),
        ((UNIT, 96, PAIRS), F32),
        ((UNIT, 96, PAIRS), F32),
        ((UNIT, 96, PAIRS), F32),
        ((UNIT, 96, PAIRS), BF16),
        ((UNIT, 128, PAIRS), F32),
        ((UNIT, 128, PAIRS), F32),
        ((UNIT, 32, PAIRS), F32),
        ((UNIT, 32, PAIRS), F32),
        ((UNIT, 16, 512), F32),
        ((UNIT, 288, 512), F32),
        ((UNIT, 96, 512), BF16),
        ((UNIT, 2, 96, 256), BF16),
        ((UNIT, 144, 128), BF16),
        ((UNIT, 288, 128), BF16),
        ((UNIT, 2, 256, 384), BF16),
        ((UNIT, 1, PAIRS), F32),
        ((UNIT, 96, 512), F32),
        ((UNIT, 288, 512), BF16),
        ((UNIT, 2, 32, 256), BF16),
        ((UNIT, 128, 256), BF16),
    ]
    return pl.pallas_call(
        pair_kernel,
        out_shape=[
            jax.ShapeDtypeStruct((sites // GROUP, GROUP), F32),
            jax.ShapeDtypeStruct((3, 768), F32),
            jax.ShapeDtypeStruct((3, 192), F32),
            jax.ShapeDtypeStruct((3, 192), F32),
        ],
        in_specs=[sm] + [vm] * 17,
        out_specs=[vm] * 4,
        scratch_shapes=[pltpu.VMEM(shape, dtype) for shape, dtype in scratch],
        compiler_params=pltpu.CompilerParams(vmem_limit_bytes=48 * 1024 * 1024),
        name="pair_terms",
    )(blocks, mid, low, high, neighbors, used, embed, first, env, latent, mix[0], out, vector.reshape(1, -1), *consts)


def shift_pairs(axis, by):
    count = lax.axis_size(axis)
    return [(i, (i + by) % count) for i in range(count)]


def on_device(positions, species, neighbors, slot_used, *params):
    sites = species.shape[-1]
    near = neighbors.reshape(sites, SLOTS)
    used = slot_used.reshape(sites, SLOTS)
    own = jnp.concatenate(
        [positions.reshape(3, sites), species.reshape(1, sites).astype(F32)], axis=0
    )
    up_x, down_x = shift_pairs("gx", 1), shift_pairs("gx", -1)
    up_y, down_y = shift_pairs("yz", 1), shift_pairs("yz", -1)
    before = lax.ppermute(own[:, 384:512], "gx", up_x)
    after = lax.ppermute(own[:, 0:128], "gx", down_x)
    mid = jnp.concatenate([before, own, after], axis=1)
    planes = mid.reshape(4, 12, 64)
    low = lax.ppermute(planes[:, :, 48:64].reshape(4, 192), "yz", up_y)
    high = lax.ppermute(planes[:, :, 0:16].reshape(4, 192), "yz", down_y)
    filled = jnp.max(jnp.where(used > 0, lax.broadcasted_iota(jnp.int32, used.shape, 0) + 1, 0))
    blocks = ((filled + GROUP - 1) // GROUP).reshape(1)
    energy, fmid, flow, fhigh = pair_call(blocks, mid, low, high, near, used, params)
    from_high = lax.ppermute(flow, "yz", down_y).reshape(3, 12, 16)
    from_low = lax.ppermute(fhigh, "yz", up_y).reshape(3, 12, 16)
    gap = jnp.zeros((3, 12, 32), F32)
    column = fmid + jnp.concatenate([from_low, gap, from_high], axis=2).reshape(3, 768)
    from_after = lax.ppermute(column[:, 0:128], "gx", down_x)
    from_before = lax.ppermute(column[:, 640:768], "gx", up_x)
    gap = jnp.zeros((3, 256), F32)
    forces = column[:, 128:640] + jnp.concatenate([from_before, gap, from_after], axis=1)
    return (energy.reshape(1, 1, sites), forces.reshape(3, 1, 1, sites))


def solution(mesh):
    in_specs = (
        P(None, "gx", "yz", None),
        P("gx", "yz", None),
        P("gx", "yz", None, None),
        P("gx", "yz", None, None),
        P(),
        P(),
        P(),
        P(),
        P(),
        P(),
        P(),
    )
    out_specs = (P("gx", "yz", None), P(None, "gx", "yz", None))
    return jax.shard_map(
        on_device, mesh=mesh, in_specs=in_specs, out_specs=out_specs, check_vma=False
    )
```

time: 1260 us -> 151 us (0.12)
  the two profiles are of different devices: /device:TPU:1 before, /device:TPU:31 now
where the time goes in v1:
time: 151 us; the launch traced here: 149 us
  Pallas kernels  119 us (79%)
  waiting for transfers between devices  15.1 us (10%)
  starting transfers between devices  7.83 us (5%)
  local copies, waits for them, and re-layouts  5.14 us (3%)
  between operations  1.55 us (1%)
    pallas_call x1, Pallas kernels, pair_call(): pl.pallas_call(pair_kernel, out_shape=[jax.ShapeDtypeStruct((sites // GRO...  119 us
    ppermute x1, starting transfers between devices, on_device(): before = lax.ppermute(own[:, 384:512], 'gx', up_x)  4.23 us
    ppermute x1, waiting for transfers between devices, on_device(): from_high = lax.ppermute(flow, 'yz', down_y).reshape(3, 12, 16)  4.22 us
    unnamed x34, local copies, waits for them, and re-layouts  3.82 us
    ppermute x1, waiting for transfers between devices, on_device(): after = lax.ppermute(own[:, 0:128], 'gx', down_x)  3.48 us
    ppermute x1, waiting for transfers between devices, on_device(): from_after = lax.ppermute(column[:, 0:128], 'gx', down_x)  3.41 us
    ppermute x1, waiting for transfers between devices, on_device(): high = lax.ppermute(planes[:, :, 0:16].reshape(4, 192), 'yz', down_y)  3.07 us
  transfers between devices with their start and end apart: 8, of which 5 were waited for; matrix products, arithmetic and copies ran while one was open for 2% of the time, Pallas kernels for 0%

profile of v1, /device:TPU:31, one launch (start us, length us, event | category | flops | bytes accessed | tf_op | source)
XLA Modules:
  0.0 149.2 jit_solution(9446299811483558951)
XLA Ops:
  0.6 0.0 copy-start.13
  0.6 0.7 copy.30
  1.3 0.0 copy-done.13
  1.4 4.2 %collective-permute-start = (f32[4,128]{1,0:T(4,128)S(1)}, f32[4,128]{1,0:T(4,128)S(1)}, u32[]{:S(2)}, u32[]{:S(2)}) collective-permute-start(f32[4,128]{1,0:T(4,128)S(1)} %get-tuple-element.18), channel_id=1, source_target_pairs={{0,32},{32,64},{64,96},{96,0},{1,33},{33,65},{65,97},{97,1},{2,34}... | collective-permute-start | bytes 6152 | tf_op jit(solution)/shard_map/ppermute | solution.py:716
  5.6 0.0 collective-permute-start.1
  5.6 1.0 copy.23
  6.6 0.0 collective-permute-done
  6.6 3.5 %collective-permute-done.1 = f32[4,128]{1,0:T(4,128)S(1)} collective-permute-done((f32[4,128]{1,0:T(4,128)S(1)}, f32[4,128]{1,0:T(4,128)S(1)}, u32[]{:S(2)}, u32[]{:S(2)}) %collective-permute-start.1) | collective-permute-done | bytes 2080 | tf_op jit(solution)/shard_map/ppermute | solution.py:717
  10.1 0.1 reshape.60
  10.2 0.1 fusion.1
  10.3 0.1 reshape.61
  10.4 0.3 collective-permute-start.2
  10.7 0.1 reshape.62
  10.8 0.0 copy-start.10
  10.8 1.2 collective-permute-start.3
  12.0 0.8 select_reduce_fusion
  13.4 0.0 copy-done.10
  13.4 0.0 copy-start.11
  13.4 0.0 copy-start.12
  13.5 0.0 copy-start.1
  13.5 0.0 copy-start.2
  13.5 0.0 copy-start.3
  13.5 0.0 copy-start.4
  13.5 0.0 copy-start.6
  13.5 0.0 copy-start.7
  13.5 0.0 copy-start.8
  13.5 0.1 copy.24
  13.7 0.5 copy-done.11
  14.2 0.0 copy-start
  14.2 0.1 copy.26.env_ref
  14.3 0.0 copy-done.12
  14.3 0.0 copy-start.5
  14.3 0.1 copy.25.first_ref
  14.4 0.0 collective-permute-done.2.low_ref
  14.4 3.1 %collective-permute-done.3.high_ref = f32[4,192]{1,0:T(4,128)S(1)} collective-permute-done((f32[4,192]{1,0:T(4,128)S(1)}, f32[4,192]{1,0:T(4,128)S(1)}, u32[]{:S(2)}, u32[]{:S(2)}) %collective-permute-start.3) | collective-permute-done | bytes 3104 | tf_op jit(solution)/shard_map/ppermute | solution.py:721
  17.5 0.0 copy-start.9
  17.5 0.0 copy-done.1
  17.5 0.0 copy-done.2
  17.5 0.0 copy-done.3
  17.5 0.0 copy-done.4
  17.5 0.0 copy-done.6
  17.5 0.0 copy-done.7
  17.6 0.0 copy-done.8
  17.6 0.0 copy-done
  17.6 0.0 copy-done.5
  17.6 0.6 copy-done.9
  18.2 118.7 %pair_terms.1 = (f32[32,16]{1,0:T(8,128)S(1)}, f32[3,768]{1,0:T(4,128)S(1)}, f32[3,192]{1,0:T(4,128)S(1)}, f32[3,192]{1,0:T(4,128)S(1)}) custom-call(s32[1]{0:T(128)} %bitcast.1.blocks_ref, f32[4,768]{1,0:T(4,128)S(1)} %pad_maximum_fusion.1.mid_ref, f32[4,192]{1,0:T(4,128)S(1)} %collective-permute-done.2.low_ref, ...), custom_call_target="tpu_custom_call" | custom-call | tf_op jit(solution)/shard_map/pair_terms/pallas_call | solution.py:686
  136.8 0.0 collective-permute-start.4
  136.9 1.5 collective-permute-start.5
  138.3 0.1 pad.4.clone
  138.4 0.9 collective-permute-done.4
  139.3 0.1 reshape.66
  139.4 4.2 %collective-permute-done.5 = f32[3,192]{1,0:T(4,128)S(1)} collective-permute-done((f32[3,192]{1,0:T(4,128)S(1)}, f32[3,192]{1,0:T(4,128)S(1)}, u32[]{:S(2)}, u32[]{:S(2)}) %collective-permute-start.5) | collective-permute-done | bytes 2336 | tf_op jit(solution)/shard_map/ppermute | solution.py:725
  143.6 0.1 reshape.67
  143.7 0.1 pad_maximum_fusion
  143.8 0.1 reshape.68
  143.9 0.1 collective-permute-start.6
  144.0 0.5 collective-permute-start.7
  144.5 0.7 reshape.65
  145.1 0.0 collective-permute-done.6
  145.1 3.4 %collective-permute-done.7 = f32[3,128]{1,0:T(4,128)S(1)} collective-permute-done((f32[3,128]{1,0:T(4,128)S(1)}, f32[3,128]{1,0:T(4,128)S(1)}, u32[]{:S(2)}, u32[]{:S(2)}) %collective-permute-start.7) | collective-permute-done | bytes 1568 | tf_op jit(solution)/shard_map/ppermute | solution.py:729
  148.6 0.6 copy.27
  (10 shorter events, 0.1 us)
Async XLA Ops:
  0.6 0.7 copy-start.13
  1.4 5.3 %collective-permute-start = (f32[4,128]{1,0:T(4,128)S(1)}, f32[4,128]{1,0:T(4,128)S(1)}, u32[]{:S(2)}, u32[]{:S(2)}) collective-permute-start(f32[4,128]{1,0:T(4,128)S(1)} %get-tuple-element.18), channel_id=1, source_target_pairs={{0,32},{32,64},{64,96},{96,0},{1,33},{33,65},{65,97},{97,1},{2,34}... | collective-permute-start | bytes 6152 | tf_op jit(solution)/shard_map/ppermute | solution.py:716
  5.6 4.5 %collective-permute-start.1 = (f32[4,128]{1,0:T(4,128)S(1)}, f32[4,128]{1,0:T(4,128)S(1)}, u32[]{:S(2)}, u32[]{:S(2)}) collective-permute-start(f32[4,128]{1,0:T(4,128)S(1)} %get-tuple-element.19), channel_id=1, source_target_pairs={{0,96},{32,0},{64,32},{96,64},{1,97},{33,1},{65,33},{97,65},{2,98}... | collective-permute-start | bytes 6152 | tf_op jit(solution)/shard_map/ppermute | solution.py:717
  10.4 4.1 %collective-permute-start.2 = (f32[4,192]{1,0:T(4,128)S(1)}, f32[4,192]{1,0:T(4,128)S(1)}, u32[]{:S(2)}, u32[]{:S(2)}) collective-permute-start(f32[4,192]{1,0:T(4,128)S(1)} %reshape.61), channel_id=1, source_target_pairs={{0,1},{1,2},{2,3},{3,4},{4,5},{5,6},{6,7},{7,8},{8,9},{9,10},{10,1... | collective-permute-start | bytes 9224 | tf_op jit(solution)/shard_map/ppermute | solution.py:720
  10.8 2.7 %copy-start.10 = (s32[1,1,512,48]{2,3,1,0:T(8,128)S(1)}, s32[1,1,512,48]{2,3,1,0:T(8,128)}, u32[]{:S(2)}) copy-start(s32[1,1,512,48]{2,3,1,0:T(8,128)} %param.18) | copy-start | bytes 294916
  10.8 6.7 %collective-permute-start.3 = (f32[4,192]{1,0:T(4,128)S(1)}, f32[4,192]{1,0:T(4,128)S(1)}, u32[]{:S(2)}, u32[]{:S(2)}) collective-permute-start(f32[4,192]{1,0:T(4,128)S(1)} %reshape.62), channel_id=1, source_target_pairs={{0,31},{1,0},{2,1},{3,2},{4,3},{5,4},{6,5},{7,6},{8,7},{9,8},{10,9... | collective-permute-start | bytes 9224 | tf_op jit(solution)/shard_map/ppermute | solution.py:721
  13.4 0.7 copy-start.11
  13.4 0.8 copy-start.12
  13.5 4.1 %copy-start.1 = (f32[96,144]{1,0:T(8,128)S(1)}, f32[96,144]{1,0:T(8,128)}, u32[]{:S(2)}) copy-start(f32[96,144]{1,0:T(8,128)} %constant.41.clone.degree_mask_ref) | copy-start | bytes 165892
  13.5 4.0 %copy-start.2 = (bf16[48,768]{1,0:T(8,128)(2,1)S(1)}, bf16[48,768]{1,0:T(8,128)(2,1)}, u32[]{:S(2)}) copy-start(bf16[48,768]{1,0:T(8,128)(2,1)} %constant.38.clone.slot_pick_ref) | copy-start | bytes 221188
  13.5 4.0 %copy-start.3 = (bf16[128,128]{1,0:T(8,128)(2,1)S(1)}, bf16[128,128]{1,0:T(8,128)(2,1)}, u32[]{:S(2)}) copy-start(bf16[128,128]{1,0:T(8,128)(2,1)} %out_ref.1) | copy-start | bytes 98308
  13.5 4.0 %copy-start.4 = (bf16[32,512]{1,0:T(8,128)(2,1)S(1)}, bf16[32,512]{1,0:T(8,128)(2,1)}, u32[]{:S(2)}) copy-start(bf16[32,512]{1,0:T(8,128)(2,1)} %constant.40.clone.chan_wide_ref) | copy-start | bytes 98308
  13.5 4.0 %copy-start.6 = (bf16[16,768]{1,0:T(8,128)(2,1)S(1)}, bf16[16,768]{1,0:T(8,128)(2,1)}, u32[]{:S(2)}) copy-start(bf16[16,768]{1,0:T(8,128)(2,1)} %constant.37.clone.atom_mask_ref) | copy-start | bytes 73732
  13.5 4.0 %copy-start.7 = (bf16[16,512]{1,0:T(8,128)(2,1)S(1)}, bf16[16,512]{1,0:T(8,128)(2,1)}, u32[]{:S(2)}) copy-start(bf16[16,512]{1,0:T(8,128)(2,1)} %constant.39.clone.atom_wide_ref) | copy-start | bytes 49156
  13.5 4.0 %copy-start.8 = (bf16[24,128]{1,0:T(8,128)(2,1)S(1)}, bf16[24,128]{1,0:T(8,128)(2,1)}, u32[]{:S(2)}) copy-start(bf16[24,128]{1,0:T(8,128)(2,1)} %embed_ref.1) | copy-start | bytes 18436
  14.2 3.4 %copy-start = (bf16[2,224,128]{2,1,0:T(8,128)(2,1)S(1)}, bf16[2,224,128]{2,1,0:T(8,128)(2,1)}, u32[]{:S(2)}) copy-start(bf16[2,224,128]{2,1,0:T(8,128)(2,1)} %latent_ref.1) | copy-start | bytes 344068
  14.3 3.3 %copy-start.5 = (bf16[1,3,32,32]{3,2,1,0:T(8,128)(2,1)S(1)}, bf16[1,3,32,32]{3,2,1,0:T(8,128)(2,1)}, u32[]{:S(2)}) copy-start(bf16[1,3,32,32]{3,2,1,0:T(8,128)(2,1)} %param.24) | copy-start | bytes 18436
  17.5 0.7 copy-start.9
  136.8 2.5 %collective-permute-start.4 = (f32[3,192]{1,0:T(4,128)S(1)}, f32[3,192]{1,0:T(4,128)S(1)}, u32[]{:S(2)}, u32[]{:S(2)}) collective-permute-start(f32[3,192]{1,0:T(4,128)S(1)} %get-tuple-element.8), channel_id=1, source_target_pairs={{0,1},{1,2},{2,3},{3,4},{4,5},{5,6},{6,7},{7,8},{8,9},{9,10},{10,1... | collective-permute-start | bytes 6920 | tf_op jit(solution)/shard_map/ppermute | solution.py:726
  136.9 6.7 %collective-permute-start.5 = (f32[3,192]{1,0:T(4,128)S(1)}, f32[3,192]{1,0:T(4,128)S(1)}, u32[]{:S(2)}, u32[]{:S(2)}) collective-permute-start(f32[3,192]{1,0:T(4,128)S(1)} %get-tuple-element.9), channel_id=1, source_target_pairs={{0,31},{1,0},{2,1},{3,2},{4,3},{5,4},{6,5},{7,6},{8,7},{9,8},{10,9... | collective-permute-start | bytes 6920 | tf_op jit(solution)/shard_map/ppermute | solution.py:725
  143.9 1.3 collective-permute-start.6
  144.0 4.6 %collective-permute-start.7 = (f32[3,128]{1,0:T(4,128)S(1)}, f32[3,128]{1,0:T(4,128)S(1)}, u32[]{:S(2)}, u32[]{:S(2)}) collective-permute-start(f32[3,128]{1,0:T(4,128)S(1)} %get-tuple-element.17), channel_id=1, source_target_pairs={{0,96},{32,0},{64,32},{96,64},{1,97},{33,1},{65,33},{97,65},{2,98}... | collective-permute-start | bytes 4616 | tf_op jit(solution)/shard_map/ppermute | solution.py:729

commit v2 on v1

--- a/solution.py
+++ b/solution.py
@@ -17,9 +17,14 @@
 SLOTS = 48
 GROUP = 16
 PAIRS = GROUP * SLOTS
-UNIT = 2
-CHUNK = 8
+UNIT = 7
+CHUNK = UNIT
 TILE = 256
+KEPT = 14
+LENT = 6
+LIGHT_BLOCKS = 8
+SHARE = 144
+BOX = 2304
 NORM = 1.0 / math.sqrt(SLOTS)
 RADIAL_GAIN = math.sqrt(2.0 / 5.0)
 DEGREES = ((0,), (1, 2, 3), (4, 5, 6, 7, 8))
@@ -37,6 +42,10 @@
 
 def tn(a, b):
     return lax.dot_general(a, b, (((0,), (0,)), ((), ())), preferred_element_type=F32)
+
+
+def eighth(value):
+    return jnp.sum(value.reshape(value.shape[0] // 8, 8, value.shape[1]), axis=0)
 
 
 def pieces(value, count):
@@ -169,6 +178,8 @@
     high_ref,
     neighbors_ref,
     used_ref,
+    lent_ref,
+    lent_sites_ref,
     embed_ref,
     first_ref,
     env_ref,
@@ -185,6 +196,8 @@
     fmid_ref,
     flow_ref,
     fhigh_ref,
+    flent_ref,
+    codes,
     far_tab,
     own_tab,
     ftab,
@@ -197,8 +210,6 @@
     mix_t,
     mix_all,
     mix_wide,
-    we_all,
-    env1,
     vec_b,
     hot,
     gat,
@@ -207,7 +218,6 @@
     geo,
     x0,
     hbd,
-    lat,
     dd,
     ss,
     j0,
@@ -219,7 +229,6 @@
     a_s,
     r_s,
     ds_b,
-    dl,
     t_s,
     small,
     dwr,
@@ -235,11 +244,13 @@
     outer,
     de_b,
     left,
+    dzs,
+    back_w,
 ):
     def turned(value):
         return value.astype(F32).T
 
-    for ref in (embed_t, l1_t, l2_t, mix_t, mix_all, we_all, env1, eb, e0t, e1r, de_b):
+    for ref in (embed_t, l1_t, l2_t, mix_t, mix_all, back_w, eb, e0t, e1r, de_b):
         ref[...] = jnp.zeros_like(ref)
     embed_t[:, 0:24] = (turned(embed_ref[...]) * 0.5).astype(BF16)
     we_t[0:32, :] = turned(first_ref[...]).astype(BF16)
@@ -248,15 +259,17 @@
     l1_t[:, 0:224] = (turned(latent_ref[0]) * 0.5).astype(BF16)
     l2_t[:, 0:224] = (turned(latent_ref[1]) * 0.5).astype(BF16)
     out_t[...] = (turned(out_ref[...]) * 0.5).astype(BF16)
-    we_all[:, 0:64] = jnp.concatenate([first_ref[...], env_ref[0]], axis=1)
-    env1[:, 0:32] = env_ref[1]
+    back_w[:, 0:480] = jnp.concatenate(
+        [out_ref[...], latent_ref[1, 0:128], env_ref[1], latent_ref[0, 0:128], first_ref[...], env_ref[0]],
+        axis=1,
+    )
     mix_all[:, 0:96] = jnp.concatenate([mix_ref[d] for d in range(3)], axis=1)
     for d in range(3):
         mix_t[32 * d : 32 * d + 32, 0:32] = turned(mix_ref[d]).astype(BF16)
     mix_wide[...] = nn(mix_t[:, 0:32], chan_wide_ref[...])
     vec_b[...] = jnp.broadcast_to(vector_ref[...].T, (128, TILE))
 
-    def enter(values_ref, per_plane, first_y):
+    def enter(values_ref, per_plane, first_y, planes=12, first_row=0):
         count = values_ref.shape[1]
         lane = lax.broadcasted_iota(jnp.int32, (1, count), 1)
         plane = lane // per_plane
@@ -270,14 +283,17 @@
         places = jnp.concatenate(pieces(xyz, 3) + lattice, axis=0)
         far = jnp.concatenate([places, kind, nil, one, nil], axis=0).T.astype(BF16)
         own = jnp.concatenate([-places, nil, kind, nil, nil], axis=0).T.astype(BF16)
-        for p in range(12):
-            start = p * 96 + first_y * LZ
+        for p in range(planes):
+            start = first_row + p * 96 + first_y * LZ
             far_tab[start : start + per_plane, :] = far[p * per_plane : (p + 1) * per_plane, :]
             own_tab[start : start + per_plane, :] = own[p * per_plane : (p + 1) * per_plane, :]
 
     enter(mid_ref, 64, 2)
     enter(low_ref, 16, 0)
     enter(high_ref, 16, 10)
+    enter(lent_sites_ref, 96, 0, 6, 1152)
+    codes[0:512, :] = jnp.where(used_ref[...] > 0, neighbors_ref[...], -1)
+    codes[512:608, :] = lent_ref[...].astype(jnp.int32)
     ftab[...] = jnp.zeros_like(ftab)
     energy_ref[...] = jnp.zeros_like(energy_ref)
     gat[...] = jnp.zeros_like(gat)
@@ -287,14 +303,25 @@
     halves = [slice(0, 384), slice(384, 768)]
     wides = [slice(0, 256), slice(256, 512)]
 
-    def row_base(block):
-        return (block // 4) * 96 + (block % 4) * 16
+    own_blocks, lent_blocks, lent_first = blocks_ref[0], blocks_ref[1], blocks_ref[2]
+
+    def place(block):
+        step = block - own_blocks
+        lent = step >= 0
+        step = jnp.minimum(step, LENT - 1)
+        home = jnp.where(lent, lent_first + step, block)
+        plane = home // 4 - jnp.where(lent, lent_first // 4 - 12, 0)
+        base = plane * 96 + (home % 4) * 16
+        row = jnp.where(block < own_blocks + lent_blocks, jnp.where(lent, 32 + step, home), 39)
+        return home, base, jnp.where(lent, 512 + step * GROUP, home * GROUP), row
 
     def fetch(block, slot):
-        x = block // 4
-        yb = block % 4
-        rows = pl.ds(pl.multiple_of(block * GROUP, GROUP), GROUP)
-        name = neighbors_ref[rows, :]
+        home, base, code_row, _ = place(block)
+        x = home // 4
+        yb = home % 4
+        name = codes[pl.ds(pl.multiple_of(code_row, GROUP), GROUP), :]
+        present = (name >= 0) & (block < own_blocks + lent_blocks)
+        name = jnp.where(present, name, 0)
         side = name >> 9
         site = name & 511
         a = (side * 11) >> 5
@@ -302,16 +329,19 @@
         ex = a * 8 + (site >> 6) - 6 - x
         ey = c * 8 + ((site >> 3) & 7) - 6 - 2 * yb
         local = ex * 48 + ey * 8 + (site & 7)
-        local = jnp.where(used_ref[rows, :] > 0, local, -1)
+        local = jnp.where(present, local, -1)
         spread = nn(local.astype(F32).astype(BF16), slot_pick_ref[...])
+        yield
         index = jnp.sum(spread * atom_mask_ref[...].astype(F32), axis=0, keepdims=True)
         hot[slot, 0:240, :] = jnp.where(hot_rows == index, 1.0, 0.0).astype(BF16)
         hot[slot, 240:256, :] = atom_mask_ref[...]
-        base = row_base(block)
+        yield
         parts = [far_tab[pl.ds(pl.multiple_of(base + 96 * i, 16), 48), :] for i in range(5)]
         parts.append(own_tab[pl.ds(pl.multiple_of(base + 208, 16), 16), :])
         table = jnp.concatenate(parts, axis=0)
-        gat[slot] = tn(table, hot[slot])
+        picked = tn(table, hot[slot])
+        yield
+        gat[slot] = picked
 
     def network(block, slot):
         mask = atom_mask_ref[...].astype(F32)
@@ -340,10 +370,9 @@
             half = nn(embed_t[:, 0:32], x0[k, :, cols])
             yield
             value, slope = swish(half)
-            ss[k, 0, :, cols] = value
-            dd[k, 0, :, cols] = slope * (0.5 * env(k, cols))
+            ss[k, 0, :, cols] = value.astype(BF16)
+            dd[k, 0, :, cols] = (slope * (0.5 * env(k, cols))).astype(BF16)
             latent = value * env(k, cols)
-            lat[k, 0, :, cols] = latent
             packed = latent.astype(BF16)
             j0[k, 0:128, cols] = packed
             we = nn(we_t[...], packed)
@@ -379,10 +408,9 @@
             yield
             a_s[k, :, cols] = mixed
             value, slope = swish(half)
-            ss[k, 1, :, cols] = value
-            dd[k, 1, :, cols] = slope * (0.5 * env(k, cols))
-            latent = lat[k, 0, :, cols] + value * env(k, cols)
-            lat[k, 1, :, cols] = latent
+            ss[k, 1, :, cols] = value.astype(BF16)
+            dd[k, 1, :, cols] = (slope * (0.5 * env(k, cols))).astype(BF16)
+            latent = j0[k, 0:128, cols].astype(F32) + value * env(k, cols)
             packed = latent.astype(BF16)
             j1[k, 0:128, cols] = packed
             coeff = nn(e1_t[...], packed)
@@ -432,24 +460,24 @@
             half = nn(l2_t[:, 0:224], j1[k, :, cols])
             yield
             value, slope = swish(half)
-            ss[k, 2, :, cols] = value
-            dd[k, 2, :, cols] = slope * (0.5 * env(k, cols))
-            latent = lat[k, 1, :, cols] + value * env(k, cols)
+            ss[k, 2, :, cols] = value.astype(BF16)
+            dd[k, 2, :, cols] = (slope * (0.5 * env(k, cols))).astype(BF16)
+            latent = j1[k, 0:128, cols].astype(F32) + value * env(k, cols)
             half = nn(out_t[...], latent.astype(BF16))
             yield
             hidden, slope = swish(half)
-            weighted = hidden * vec_b[...]
+            weighted = eighth(hidden * vec_b[...])
             t_s[k, :, cols] = weighted
-            dz3 = (slope * vec_b[...] * (0.5 * env(k, cols))).astype(BF16)
-            dl2 = nn(out_ref[...], dz3)
+            dz = (slope * vec_b[...] * (0.5 * env(k, cols))).astype(BF16)
+            dzs[k, 0:128, cols] = dz
+            dl = nn(out_ref[...], dz)
             pair_energy[k, :, cols] = jnp.sum(weighted, axis=0, keepdims=True) * env(k, cols)
             yield
-            t_s[k, :, cols] = t_s[k, :, cols] + dl2 * ss[k, 2, :, cols]
-            dl[k, :, cols] = dl2
-            dj = nn(latent_ref[1], (dl2 * dd[k, 2, :, cols]).astype(BF16))
-            yield
-            dl[k, :, cols] = dl[k, :, cols] + dj[0:128]
-            dscal = dj[128:224]
+            t_s[k, :, cols] = t_s[k, :, cols] + eighth(dl * ss[k, 2, :, cols].astype(F32))
+            dz = (dl * dd[k, 2, :, cols].astype(F32)).astype(BF16)
+            dzs[k, 128:256, cols] = dz
+            dscal = nn(latent_ref[1, 128:224, :], dz)
+            yield
             ds_b[k, :, cols] = dscal.astype(BF16)
             dmix = nn(mix_all[:, 0:96], (dscal * q1_s[k, :, cols]).astype(BF16))
             dq = (dscal * a_s[k, :, cols]).astype(BF16)
@@ -463,7 +491,7 @@
             high, middle, low = pieces(row, 3)
             fill = jnp.zeros((5, PAIRS), F32)
             total = nt(jnp.concatenate([high, middle, low, fill], axis=0).astype(BF16), atom_mask_ref[...])
-            energy_ref[pl.ds(block + k, 1), :] = total[0:1] + (total[1:2] + total[2:3])
+            energy_ref[pl.ds(place(block + k)[3], 1), :] = total[0:1] + (total[1:2] + total[2:3])
             for half in range(2):
                 db[k, :, wides[half]] = nt(ds_b[k, :, halves[half]], ww[k, half])
                 back = tn(bmat[k, :, wides[half]], ds_b[k, :, halves[half]])
@@ -494,21 +522,21 @@
         def stage_f(k, cols):
             dcoeff = nn(de_b[k, 1, :, 0:144], hbd[k, :, cols])
             yield
-            more = nn(env1[:, 0:32], dcoeff.astype(BF16))
-            yield
-            dl1 = dl[k, :, cols] + more
-            t_s[k, :, cols] = t_s[k, :, cols] + dl1 * ss[k, 1, :, cols]
-            dl[k, :, cols] = dl1
-            dj = nn(latent_ref[0], (dl1 * dd[k, 1, :, cols]).astype(BF16))
-            yield
-            dl[k, :, cols] = dl[k, :, cols] + dj[0:128]
-            dscal = [dj[128:160] + small[k, :, cols], dj[160:192], dj[192:224]]
+            dzs[k, 256:288, cols] = dcoeff.astype(BF16)
+            dl = nn(back_w[:, 0:288], dzs[k, 0:288, cols])
+            yield
+            t_s[k, :, cols] = t_s[k, :, cols] + eighth(dl * ss[k, 1, :, cols].astype(F32))
+            dz = (dl * dd[k, 1, :, cols].astype(F32)).astype(BF16)
+            dzs[k, 288:416, cols] = dz
+            dscal = nn(latent_ref[0, 128:224, :], dz)
+            yield
+            dscal = [dscal[0:32] + small[k, :, cols], dscal[32:64], dscal[64:96]]
             w = w_s[k, :, cols]
             dw = dwr[k, :, cols]
             for d in range(3):
                 cat[k, 96 + 32 * d : 128 + 32 * d, cols] = (dscal[d] * w).astype(BF16)
                 dw = dw + dscal[d] * q_s[k, 32 * d : 32 * d + 32, cols]
-            dwr[k, :, cols] = dw
+            dzs[k, 416:448, cols] = dw.astype(BF16)
             gather_sum(("d0", k), nt(cat[k, 96:192, cols], hbd[k, :, cols]))
             yield
 
@@ -530,19 +558,17 @@
             dcoeff = nn(de_b[k, 0, :, 0:144], hbd[k, :, cols])
             dhbd = nn(left[k], cat[k, :, cols])
             yield
-            both = jnp.concatenate([dwr[k, :, cols], dcoeff], axis=0).astype(BF16)
-            more = nn(we_all[:, 0:64], both)
+            dzs[k, 448:480, cols] = dcoeff.astype(BF16)
+            dl = nn(back_w[:, 0:480], dzs[k, 0:480, cols])
             for i in range(8):
                 dfeat[slot + k, 8 + i : 9 + i, cols] = jnp.sum(
                     dhbd[16 * i : 16 * i + 16, :] * mask[:, cols], axis=0, keepdims=True
                 )
             yield
-            so_far = dl[k, :, cols]
-            dl0 = jnp.where(jnp.abs(so_far) < 1e30, so_far, 0.0) + more
-            dz = (dl0 * dd[k, 0, :, cols]).astype(BF16)
+            dz = (dl * dd[k, 0, :, cols].astype(F32)).astype(BF16)
             dradial = nn(embed_ref[...], dz)
             dfeat[slot + k, 16:17, cols] = jnp.sum(
-                t_s[k, :, cols] + dl0 * ss[k, 0, :, cols], axis=0, keepdims=True
+                t_s[k, :, cols] + eighth(dl * ss[k, 0, :, cols].astype(F32)), axis=0, keepdims=True
             )
             yield
             dfeat[slot + k, 0:8, cols] = dradial[0:8]
@@ -567,18 +593,18 @@
 
     def scatter(block, slot):
         pulled = nt(hot[slot], dfeat[slot, 0:16, :].astype(BF16))
-        base = row_base(block)
+        yield
+        _, base, _, _ = place(block)
         for i in range(5):
             rows = pl.ds(pl.multiple_of(base + 96 * i, 16), 48)
             ftab[rows, :] = ftab[rows, :] - pulled[48 * i : 48 * i + 48, :]
         rows = pl.ds(pl.multiple_of(base + 208, 16), 16)
         ftab[rows, :] = ftab[rows, :] + pulled[240:256, :]
 
-    blocks = ((blocks_ref[0] + UNIT - 1) // UNIT) * UNIT
+    blocks = own_blocks + lent_blocks
 
     def chunk_step(chunk, carry):
         first = chunk * CHUNK
-        count = jnp.minimum(CHUNK, blocks - first)
 
         def rows_of(ref):
             return lambda f: jnp.concatenate([ref[b, f : f + 1, :] for b in range(CHUNK)], axis=0)
@@ -590,25 +616,22 @@
 
             return put
 
-        def each(step, size=1):
-            def turn(i, c):
-                step(first + i * size, i * size)
-                return c
-
-            lax.fori_loop(0, (count + size - 1) // size, turn, 0)
-
-        each(fetch)
+        together([fetch(first + k, k) for k in range(UNIT)])
         geometry(rows_of(gat), rows_to(feat), geo)
-        each(network, UNIT)
+        network(first, 0)
         geometry_back(rows_of(dfeat), rows_to(dfeat), geo)
-        each(scatter)
+        together([scatter(first + k, k) for k in range(UNIT)])
         return carry
 
     lax.fori_loop(0, (blocks + CHUNK - 1) // CHUNK, chunk_step, 0)
 
-    def leave(force_ref, per_plane, first_y):
+    def leave(force_ref, per_plane, first_y, planes=12, first_row=0):
         rows = jnp.concatenate(
-            [ftab[p * 96 + first_y * LZ : p * 96 + first_y * LZ + per_plane, :] for p in range(12)], axis=0
+            [
+                ftab[first_row + p * 96 + first_y * LZ : first_row + p * 96 + first_y * LZ + per_plane, :]
+                for p in range(planes)
+            ],
+            axis=0,
         )
         turned_rows = rows.T
         force_ref[...] = turned_rows[0:3] + turned_rows[3:6]
@@ -616,9 +639,10 @@
     leave(fmid_ref, 64, 2)
     leave(flow_ref, 16, 0)
     leave(fhigh_ref, 16, 10)
-
-
-def pair_call(blocks, mid, low, high, neighbors, used, params):
+    leave(flent_ref, 96, 0, 6, 1152)
+
+
+def pair_call(blocks, mid, low, high, neighbors, used, lent, lent_sites, params):
     embed, first, env, latent, mix, out, vector = params
     sites = neighbors.shape[0]
     atom_mask, slot_pick, atom_wide, chan_wide, degree_mask = constants()
@@ -632,9 +656,10 @@
     vm = pl.BlockSpec(memory_space=pltpu.VMEM)
     sm = pl.BlockSpec(memory_space=pltpu.SMEM)
     scratch = [
-        ((1152, 16), BF16),
-        ((1152, 16), BF16),
-        ((1152, 16), F32),
+        ((608, SLOTS), jnp.int32),
+        ((1728, 16), BF16),
+        ((1728, 16), BF16),
+        ((1728, 16), F32),
         ((128, 128), BF16),
         ((64, 128), BF16),
         ((128, 256), BF16),
@@ -644,8 +669,6 @@
         ((96, 128), BF16),
         ((32, 128), BF16),
         ((96, 512), F32),
-        ((128, 128), BF16),
-        ((128, 128), BF16),
         ((128, TILE), F32),
         ((CHUNK, 256, PAIRS), BF16),
         ((CHUNK, 16, PAIRS), F32),
@@ -654,9 +677,8 @@
         ((14, CHUNK, PAIRS), F32),
         ((UNIT, 32, PAIRS), BF16),
         ((UNIT, 144, PAIRS), BF16),
-        ((UNIT, 2, 128, PAIRS), F32),
-        ((UNIT, 3, 128, PAIRS), F32),
-        ((UNIT, 3, 128, PAIRS), F32),
+        ((UNIT, 3, 128, PAIRS), BF16),
+        ((UNIT, 3, 128, PAIRS), BF16),
         ((UNIT, 224, PAIRS), BF16),
         ((UNIT, 224, PAIRS), BF16),
         ((UNIT, 32, PAIRS), F32),
@@ -666,8 +688,7 @@
         ((UNIT, 96, PAIRS), F32),
         ((UNIT, 96, PAIRS), F32),
         ((UNIT, 96, PAIRS), BF16),
-        ((UNIT, 128, PAIRS), F32),
-        ((UNIT, 128, PAIRS), F32),
+        ((UNIT, 8, PAIRS), F32),
         ((UNIT, 32, PAIRS), F32),
         ((UNIT, 32, PAIRS), F32),
         ((UNIT, 16, 512), F32),
@@ -682,37 +703,108 @@
         ((UNIT, 288, 512), BF16),
         ((UNIT, 2, 32, 256), BF16),
         ((UNIT, 128, 256), BF16),
+        ((UNIT, 480, PAIRS), BF16),
+        ((128, 512), BF16),
     ]
     return pl.pallas_call(
         pair_kernel,
         out_shape=[
-            jax.ShapeDtypeStruct((sites // GROUP, GROUP), F32),
+            jax.ShapeDtypeStruct((sites // GROUP + 8, GROUP), F32),
             jax.ShapeDtypeStruct((3, 768), F32),
             jax.ShapeDtypeStruct((3, 192), F32),
             jax.ShapeDtypeStruct((3, 192), F32),
+            jax.ShapeDtypeStruct((3, 576), F32),
         ],
-        in_specs=[sm] + [vm] * 17,
-        out_specs=[vm] * 4,
+        in_specs=[sm] + [vm] * 19,
+        out_specs=[vm] * 5,
         scratch_shapes=[pltpu.VMEM(shape, dtype) for shape, dtype in scratch],
         compiler_params=pltpu.CompilerParams(vmem_limit_bytes=48 * 1024 * 1024),
         name="pair_terms",
-    )(blocks, mid, low, high, neighbors, used, embed, first, env, latent, mix[0], out, vector.reshape(1, -1), *consts)
-
-
-def shift_pairs(axis, by):
+    )(blocks, mid, low, high, neighbors, used, lent, lent_sites, embed, first, env, latent, mix[0], out, vector.reshape(1, -1), *consts)
+
+
+def route_kernel(me_ref, shares_ref, boxes_ref, forward_ref, lender_ref, blocks_ref):
+    count = shares_ref.shape[0]
+    me = me_ref[0]
+    down = lax.broadcasted_iota(jnp.int32, (count, count), 0)
+    right = lax.broadcasted_iota(jnp.int32, (count, count), 1)
+    need = shares_ref[:, 3 * SHARE : 3 * SHARE + 1]
+    need_down = jnp.broadcast_to(need, (count, count))
+    need_right = jnp.sum(jnp.where(down == right, need_down, 0.0), axis=0, keepdims=True)
+    need_right = jnp.broadcast_to(need_right, (count, count))
+    full_down = need_down > LIGHT_BLOCKS + 0.5
+    full_right = need_right > LIGHT_BLOCKS + 0.5
+    rank_down = jnp.sum(jnp.where(full_right & (right < down), 1.0, 0.0), axis=1, keepdims=True)
+    rank_down = jnp.broadcast_to(rank_down, (count, count))
+    rank_right = jnp.sum(jnp.where(full_down & (down < right), 1.0, 0.0), axis=0, keepdims=True)
+    rank_right = jnp.broadcast_to(rank_right, (count, count))
+    light_down = jnp.where(full_down, -1.0, down.astype(F32) - rank_down)
+    light_right = jnp.where(full_right, -1.0, right.astype(F32) - rank_right)
+    lends_right = jnp.where(full_right, 3.0 * rank_right, 1000.0)
+    lends_down = jnp.where(full_down, 3.0 * rank_down, 1000.0)
+    total = jnp.zeros((count, SHARE), F32)
+    boxes = jnp.zeros((count, BOX), F32)
+    lender = jnp.zeros((count, 1), F32)
+    parts = jnp.zeros((count, 1), F32)
+    for j in range(3):
+        choice = jnp.where(light_down == lends_right + j, 1.0, 0.0)
+        names = shares_ref[:, j * SHARE : (j + 1) * SHARE]
+        high, low = pieces(names, 2)
+        choice_b = choice.astype(BF16)
+        total = total + (nn(choice_b, high.astype(BF16)) + nn(choice_b, low.astype(BF16)))
+        mine = jnp.sum(jnp.where(right == me, choice, 0.0), axis=1, keepdims=True)
+        boxes = boxes + mine * boxes_ref[j : j + 1, :]
+        taken = jnp.where((light_right == lends_down + j) & (right == me), 1.0, 0.0)
+        taken = jnp.sum(taken, axis=1, keepdims=True)
+        lender = lender + taken
+        parts = parts + j * taken
+    forward_ref[:, 0:SHARE] = total
+    forward_ref[:, SHARE : SHARE + BOX] = boxes
+    lender_ref[...] = lender
+    here = lax.broadcasted_iota(jnp.int32, (count, 1), 0) == me
+    own_need = jnp.sum(jnp.where(here, need, 0.0)).astype(jnp.int32)
+    lent_need = jnp.sum(lender * need).astype(jnp.int32)
+    part = jnp.sum(parts).astype(jnp.int32)
+    first = KEPT + LENT * part
+    blocks_ref[0] = jnp.where(own_need > LIGHT_BLOCKS, jnp.minimum(own_need, KEPT), own_need)
+    blocks_ref[1] = jnp.minimum(jnp.maximum(lent_need - first, 0), LENT)
+    blocks_ref[2] = first
+    blocks_ref[3] = part
+
+
+def route_call(me, shares, boxes):
+    count = shares.shape[0]
+    vm = pl.BlockSpec(memory_space=pltpu.VMEM)
+    sm = pl.BlockSpec(memory_space=pltpu.SMEM)
+    return pl.pallas_call(
+        route_kernel,
+        out_shape=[
+            jax.ShapeDtypeStruct((count, SHARE + BOX), F32),
+            jax.ShapeDtypeStruct((count, 1), F32),
+            jax.ShapeDtypeStruct((4,), jnp.int32),
+        ],
+        in_specs=[sm, vm, vm],
+        out_specs=[vm, vm, sm],
+        name="route",
+    )(me, shares, boxes)
+
+
+def ring(axis, by):
     count = lax.axis_size(axis)
     return [(i, (i + by) % count) for i in range(count)]
 
 
 def on_device(positions, species, neighbors, slot_used, *params):
     sites = species.shape[-1]
+    count = lax.axis_size("yz")
+    me = lax.axis_index("yz")
     near = neighbors.reshape(sites, SLOTS)
     used = slot_used.reshape(sites, SLOTS)
     own = jnp.concatenate(
         [positions.reshape(3, sites), species.reshape(1, sites).astype(F32)], axis=0
     )
-    up_x, down_x = shift_pairs("gx", 1), shift_pairs("gx", -1)
-    up_y, down_y = shift_pairs("yz", 1), shift_pairs("yz", -1)
+    up_x, down_x = ring("gx", 1), ring("gx", -1)
+    up_y, down_y = ring("yz", 1), ring("yz", -1)
     before = lax.ppermute(own[:, 384:512], "gx", up_x)
     after = lax.ppermute(own[:, 0:128], "gx", down_x)
     mid = jnp.concatenate([before, own, after], axis=1)
@@ -720,17 +812,62 @@
     low = lax.ppermute(planes[:, :, 48:64].reshape(4, 192), "yz", up_y)
     high = lax.ppermute(planes[:, :, 0:16].reshape(4, 192), "yz", down_y)
     filled = jnp.max(jnp.where(used > 0, lax.broadcasted_iota(jnp.int32, used.shape, 0) + 1, 0))
-    blocks = ((filled + GROUP - 1) // GROUP).reshape(1)
-    energy, fmid, flow, fhigh = pair_call(blocks, mid, low, high, near, used, params)
-    from_high = lax.ppermute(flow, "yz", down_y).reshape(3, 12, 16)
-    from_low = lax.ppermute(fhigh, "yz", up_y).reshape(3, 12, 16)
-    gap = jnp.zeros((3, 12, 32), F32)
-    column = fmid + jnp.concatenate([from_low, gap, from_high], axis=2).reshape(3, 768)
+    need = (filled + GROUP - 1) // GROUP
+
+    last = slice(KEPT * GROUP, sites)
+    codes = jnp.where(used[last] > 0, near[last], -1).astype(F32).reshape(3, count, SHARE)
+    shares = codes.transpose(1, 0, 2).reshape(count, 3 * SHARE)
+    shares = jnp.concatenate([shares, jnp.full((count, 1), need, jnp.int32).astype(F32)], axis=1)
+    shares = lax.all_to_all(shares, "yz", 0, 0, tiled=True)
+    box = jnp.concatenate([low.reshape(4, 12, 16), planes, high.reshape(4, 12, 16)], axis=2)
+    firsts = [KEPT + LENT * j for j in range(3)]
+    boxes = jnp.concatenate([box[:, f // 4 : f // 4 + 6].reshape(1, BOX) for f in firsts], axis=0)
+    forward, lender, blocks = route_call(me.astype(jnp.int32).reshape(1), shares, boxes)
+    lent = lax.all_to_all(forward, "yz", 0, 0, tiled=True)
+    lent_codes = lent[:, 0:SHARE].reshape(2 * SLOTS, SLOTS)
+    lent_sites = jnp.sum(lent[:, SHARE:] * lender, axis=0).reshape(4, 576)
+    part = blocks[3]
+
+    energy, fmid, flow, fhigh, flent = pair_call(
+        blocks, mid, low, high, near, used, lent_codes, lent_sites, params
+    )
+
+    lent_force = flent.reshape(3, 6, 96)
+    wide = sum(
+        jnp.where(part == j, jnp.pad(lent_force, ((0, 0), (f // 4, 6 - f // 4), (0, 0))), 0.0)
+        for j, f in enumerate(firsts)
+    )
+
+    def to_low(edge):
+        return jnp.pad(edge, ((0, 0), (0, 0), (48, 0))).reshape(1, -1)
+
+    def to_high(edge):
+        return jnp.pad(edge, ((0, 0), (0, 0), (0, 48))).reshape(1, -1)
+
+    device = jnp.arange(count, dtype=jnp.int32)
+    home = lender
+    home_low = jnp.roll(lender, -1, axis=0)
+    home_high = jnp.roll(lender, 1, axis=0)
+    me_low = (device == (me + count - 1) % count).astype(F32)[:, None]
+    me_high = (device == (me + 1) % count).astype(F32)[:, None]
+    sent = (
+        home * wide[:, :, 16:80].reshape(1, -1)
+        + home_low * to_low(wide[:, :, 0:16])
+        + home_high * to_high(wide[:, :, 80:96])
+        + me_low * to_low(flow.reshape(3, 12, 16))
+        + me_high * to_high(fhigh.reshape(3, 12, 16))
+    )
+    lent_energy = energy[32:38].reshape(1, 96)
+    parts = [jnp.where(part == j, home * lent_energy, 0.0) for j in range(3)]
+    got = lax.all_to_all(jnp.concatenate([sent] + parts, axis=1), "yz", 0, 0, tiled=True)
+    got = jnp.sum(got, axis=0)
+    column = fmid + got[0:2304].reshape(3, 768)
+    own_energy = energy[0:32].reshape(sites) + jnp.pad(got[2304:2592], (KEPT * GROUP, 0))
     from_after = lax.ppermute(column[:, 0:128], "gx", down_x)
     from_before = lax.ppermute(column[:, 640:768], "gx", up_x)
     gap = jnp.zeros((3, 256), F32)
     forces = column[:, 128:640] + jnp.concatenate([from_before, gap, from_after], axis=1)
-    return (energy.reshape(1, 1, sites), forces.reshape(3, 1, 1, sites))
+    return (own_energy.reshape(1, 1, sites), forces.reshape(3, 1, 1, sites))
 
 
 def solution(mesh):

time: 151 us -> 116 us (0.77)
  the two profiles are of different devices: /device:TPU:31 before, /device:TPU:1 now
where the time goes in v2:
time: 116 us
  Pallas kernels  41.4 us (36%)
  starting transfers between devices  38.1 us (33%)
  waiting for transfers between devices  14.5 us (12%)
  local copies, waits for them, and re-layouts  13.6 us (12%)
  other arithmetic  4.45 us (4%)
  between operations  3.7 us (3%)
    pallas_call x1, Pallas kernels, pair_call(): pl.pallas_call(pair_kernel, out_shape=[jax.ShapeDtypeStruct((sites // GRO...  39.3 us
    all_to_all x1, waiting for transfers between devices, on_device(): lax.all_to_all(jnp.concatenate([sent] + parts, axis=1), 'yz', 0, 0, tiled...  7.91 us
    ppermute x1, starting transfers between devices, on_device(): from_before = lax.ppermute(column[:, 640:768], 'gx', up_x)  7.9 us
    all_to_all x1, starting transfers between devices, on_device(): shares = lax.all_to_all(shares, 'yz', 0, 0, tiled=True)  7.49 us
    all_to_all x1, starting transfers between devices, on_device(): lent = lax.all_to_all(forward, 'yz', 0, 0, tiled=True)  6.89 us
    unnamed x42, local copies, waits for them, and re-layouts  5.93 us
    all_to_all x1, starting transfers between devices, on_device(): lax.all_to_all(jnp.concatenate([sent] + parts, axis=1), 'yz', 0, 0, tiled...  5.07 us
    ppermute x1, starting transfers between devices, on_device(): before = lax.ppermute(own[:, 384:512], 'gx', up_x)  5.06 us
  transfers between devices with their start and end apart: 9, of which 4 were waited for; matrix products, arithmetic and copies ran while one was open for 7% of the time, Pallas kernels for 0%

profile of v2, /device:TPU:1, one launch (start us, length us, event | category | flops | bytes accessed | tf_op | source)
XLA Modules:
  0.0 115.7 jit_solution(3041679404363772034)
XLA Ops:
  0.6 0.7 copy.52
  1.4 5.1 %collective-permute-start = (f32[4,128]{1,0:T(4,128)S(1)}, f32[4,128]{1,0:T(4,128)S(1)}, u32[]{:S(2)}, u32[]{:S(2)}) collective-permute-start(f32[4,128]{1,0:T(4,128)S(1)} %get-tuple-element.37), channel_id=1, source_target_pairs={{0,32},{32,64},{64,96},{96,0},{1,33},{33,65},{65,97},{97,1},{2,34}... | collective-permute-start | bytes 6152 | tf_op jit(solution)/shard_map/ppermute | solution.py:808
  6.4 1.0 copy.32
  7.5 0.8 select_reduce_fusion
  8.9 0.1 select_convert_fusion
  9.0 0.1 copy.30
  9.1 0.1 convert_element_type.54
  9.3 0.1 reshape.132
  9.5 0.7 copy.33
  10.1 7.5 %all-to-all-start = ((f32[32,1,433]{2,1,0:T(1,128)}), f32[32,1,433]{2,1,0:T(1,128)S(1)}, u32[]{:S(2)}, u32[]{:S(2)}) async-start(f32[32,1,433]{2,1,0:T(1,128)} %copy.33), calls=%async_computation | async-start | bytes 131072 | tf_op jit(solution)/shard_map/all_to_all | solution.py:821
  17.7 0.1 reshape.135
  17.9 0.1 reshape.136
  18.0 1.2 %collective-permute-start.2 = (f32[4,192]{1,0:T(4,128)S(1)}, f32[4,192]{1,0:T(4,128)S(1)}, u32[]{:S(2)}, u32[]{:S(2)}) collective-permute-start(f32[4,192]{1,0:T(4,128)S(1)} %reshape.136), channel_id=1, source_target_pairs={{0,1},{1,2},{2,3},{3,4},{4,5},{5,6},{6,7},{7,8},{8,9},{9,10},{10,1... | collective-permute-start | bytes 9224 | tf_op jit(solution)/shard_map/ppermute | solution.py:812
  19.2 0.1 reshape.138
  19.3 4.5 %collective-permute-start.3 = (f32[4,192]{1,0:T(4,128)S(1)}, f32[4,192]{1,0:T(4,128)S(1)}, u32[]{:S(2)}, u32[]{:S(2)}) collective-permute-start(f32[4,192]{1,0:T(4,128)S(1)} %reshape.138), channel_id=1, source_target_pairs={{0,31},{1,0},{2,1},{3,2},{4,3},{5,4},{6,5},{7,6},{8,7},{9,8},{10,9... | collective-permute-start | bytes 9224 | tf_op jit(solution)/shard_map/ppermute | solution.py:813
  23.7 0.1 copy.34
  23.9 0.6 copy-done.14
  24.5 0.1 copy.37.env_ref
  24.6 0.6 copy-done.15
  25.2 0.1 copy.36.first_ref
  25.3 0.1 reshape.137
  25.4 0.1 reshape.139
  25.4 0.1 pad_maximum_fusion.1
  25.6 0.1 reshape.140
  25.7 0.1 reshape.141
  25.7 0.1 reshape.142
  25.8 0.6 pad_maximum_fusion.boxes_ref
  26.5 0.6 copy.51
  27.1 2.1 %route.1 = (f32[32,2448]{1,0:T(8,128)}, f32[32,1]{1,0:T(8,128)}, s32[4]{0:T(128)}) custom-call(s32[1]{0:T(128)} %bitcast.me_ref, f32[32,433]{1,0:T(8,128)} %bitcast.46, f32[3,2304]{1,0:T(4,128)} %pad_maximum_fusion.boxes_ref), custom_call_target="tpu_custom_call" | custom-call | tf_op jit(solution)/shard_map/route/pallas_call | solution.py:779
  29.2 2.0 %copy.35 = f32[32,1,2448]{2,1,0:T(1,128)} copy(f32[32,1,2448]{2,0,1:T(8,128)} %bitcast.45) | data formatting | bytes 626688 | tf_op jit(solution)/shard_map/all_to_all | solution.py:826
  31.2 6.9 %all-to-all-start.1 = ((f32[32,1,2448]{2,1,0:T(1,128)}), f32[32,1,2448]{2,1,0:T(1,128)S(1)}, u32[]{:S(2)}, u32[]{:S(2)}) async-start(f32[32,1,2448]{2,1,0:T(1,128)} %copy.35), calls=%async_computation.1 | async-start | bytes 655360 | tf_op jit(solution)/shard_map/all_to_all | solution.py:826
  38.2 0.1 reduce.1
  38.3 0.7 copy-done.10
  38.9 0.6 slice.96
  41.5 0.1 copy.38
  41.5 0.1 copy.41
  41.6 0.5 fusion.6
  42.2 1.4 %maximum_bitcast_fusion = (f32[32]{0:T(128)S(1)}, f32[32]{0:T(128)S(1)}) fusion(f32[1,1]{0,1:T(1,128)} %bitcast.12, f32[31,1]{0,1:T(1,128)S(1)} %copy.38, f32[31,1]{0,1:T(1,128)S(1)} %copy.41, f32[1,1]{0,1:T(1,128)} %bitcast.14), kind=kLoop, calls=%fused_computation.26 | loop fusion | flops 64 | bytes 512 | tf_op jit(solution)/shard_map/mul | solution.py:855
  43.5 2.7 %all-to-all-done.1 = f32[32,1,2448]{2,1,0:T(1,128)S(1)} async-done(((f32[32,1,2448]{2,1,0:T(1,128)}), f32[32,1,2448]{2,1,0:T(1,128)S(1)}, u32[]{:S(2)}, u32[]{:S(2)}) %all-to-all-start.1) | async-done | bytes 313376 | tf_op jit(solution)/shard_map/all_to_all | solution.py:826
  46.3 0.2 fusion
  46.5 0.1 reshape.145.lent_sites_ref
  46.6 0.1 reshape.144.lent_ref
  46.7 0.2 copy-done.8
  46.9 0.2 copy-done
  47.2 0.2 copy-done.1
  47.4 39.3 %pair_terms.1 = (f32[40,16]{1,0:T(8,128)S(1)}, f32[3,768]{1,0:T(4,128)S(1)}, f32[3,192]{1,0:T(4,128)S(1)}, f32[3,192]{1,0:T(4,128)S(1)}, f32[3,576]{1,0:T(4,128)S(1)}) custom-call(s32[4]{0:T(128)S(1)} %copy-done.10, f32[4,768]{1,0:T(4,128)S(1)} %pad_maximum_fusion.2.mid_ref, f32[4,192]{1,0:T(4,128)S(1)} %collective-permute-done.2.low_ref, ...), custom_call_target="tpu_custom_call" | custom-call | tf_op jit(solution)/shard_map/pair_terms/pallas_call | solution.py:709
  86.7 0.1 reshape.148
  87.0 0.1 mul.141
  87.2 0.1 pad.34
  87.5 0.1 reshape.149
  87.6 0.1 pad.36
  87.7 0.1 reshape.150
  87.9 0.2 multiply_add_fusion
  88.1 0.1 concatenate.36
  88.2 1.1 copy.42
  89.3 5.1 %all-to-all-start.2 = ((f32[32,1,2592]{2,1,0:T(1,128)}), f32[32,1,2592]{2,1,0:T(1,128)S(1)}, u32[]{:S(2)}, u32[]{:S(2)}) async-start(f32[32,1,2592]{2,1,0:T(1,128)} %copy.42), calls=%async_computation.2 | async-start | bytes 688128 | tf_op jit(solution)/shard_map/all_to_all | solution.py:862
  94.4 0.1 reshape.147
  94.5 7.9 %all-to-all-done.2 = f32[32,1,2592]{2,1,0:T(1,128)S(1)} async-done(((f32[32,1,2592]{2,1,0:T(1,128)}), f32[32,1,2592]{2,1,0:T(1,128)S(1)}, u32[]{:S(2)}, u32[]{:S(2)}) %all-to-all-start.2) | async-done | bytes 331808 | tf_op jit(solution)/shard_map/all_to_all | solution.py:862
  102.4 0.2 reduce_sum.19
  102.7 7.9 %collective-permute-start.4 = (f32[3,128]{1,0:T(4,128)S(1)}, f32[3,128]{1,0:T(4,128)S(1)}, u32[]{:S(2)}, u32[]{:S(2)}) collective-permute-start(f32[3,128]{1,0:T(4,128)S(1)} %get-tuple-element.35), channel_id=1, source_target_pairs={{0,32},{32,64},{64,96},{96,0},{1,33},{33,65},{65,97},{97,1},{2,34}... | collective-permute-start | bytes 4616 | tf_op jit(solution)/shard_map/ppermute | solution.py:867
  110.6 0.7 pad_add_fusion
  111.2 0.1 collective-permute-done.4
  111.3 3.8 %collective-permute-done.5 = f32[3,128]{1,0:T(4,128)S(1)} collective-permute-done((f32[3,128]{1,0:T(4,128)S(1)}, f32[3,128]{1,0:T(4,128)S(1)}, u32[]{:S(2)}, u32[]{:S(2)}) %collective-permute-start.5) | collective-permute-done | bytes 1568 | tf_op jit(solution)/shard_map/ppermute | solution.py:866
  115.1 0.6 copy.43
  (67 shorter events, 1.1 us)
Async XLA Ops:
  0.6 0.7 copy-start.16
  1.4 16.3 %collective-permute-start = (f32[4,128]{1,0:T(4,128)S(1)}, f32[4,128]{1,0:T(4,128)S(1)}, u32[]{:S(2)}, u32[]{:S(2)}) collective-permute-start(f32[4,128]{1,0:T(4,128)S(1)} %get-tuple-element.37), channel_id=1, source_target_pairs={{0,32},{32,64},{64,96},{96,0},{1,33},{33,65},{65,97},{97,1},{2,34}... | collective-permute-start | bytes 6152 | tf_op jit(solution)/shard_map/ppermute | solution.py:808
  6.4 11.3 %collective-permute-start.1 = (f32[4,128]{1,0:T(4,128)S(1)}, f32[4,128]{1,0:T(4,128)S(1)}, u32[]{:S(2)}, u32[]{:S(2)}) collective-permute-start(f32[4,128]{1,0:T(4,128)S(1)} %get-tuple-element.38), channel_id=1, source_target_pairs={{0,96},{32,0},{64,32},{96,64},{1,97},{33,1},{65,33},{97,65},{2,98}... | collective-permute-start | bytes 6152 | tf_op jit(solution)/shard_map/ppermute | solution.py:809
  7.4 1.5 %copy-start.11 = (s32[1,1,512,48]{2,3,1,0:T(8,128)S(1)}, s32[1,1,512,48]{2,3,1,0:T(8,128)}, u32[]{:S(2)}) copy-start(s32[1,1,512,48]{2,3,1,0:T(8,128)} %param.19) | copy-start | bytes 294916
  7.5 1.5 %copy-start.12 = (s32[1,1,512,48]{2,3,1,0:T(8,128)S(1)}, s32[1,1,512,48]{2,3,1,0:T(8,128)}, u32[]{:S(2)}) copy-start(s32[1,1,512,48]{2,3,1,0:T(8,128)} %param.18) | copy-start | bytes 294916
  10.1 16.3 %all-to-all-start = ((f32[32,1,433]{2,1,0:T(1,128)}), f32[32,1,433]{2,1,0:T(1,128)S(1)}, u32[]{:S(2)}, u32[]{:S(2)}) async-start(f32[32,1,433]{2,1,0:T(1,128)} %copy.33), calls=%async_computation | async-start | bytes 131072 | tf_op jit(solution)/shard_map/all_to_all | solution.py:821
  18.0 7.3 %collective-permute-start.2 = (f32[4,192]{1,0:T(4,128)S(1)}, f32[4,192]{1,0:T(4,128)S(1)}, u32[]{:S(2)}, u32[]{:S(2)}) collective-permute-start(f32[4,192]{1,0:T(4,128)S(1)} %reshape.136), channel_id=1, source_target_pairs={{0,1},{1,2},{2,3},{3,4},{4,5},{5,6},{6,7},{7,8},{8,9},{9,10},{10,1... | collective-permute-start | bytes 9224 | tf_op jit(solution)/shard_map/ppermute | solution.py:812
  19.3 6.1 %collective-permute-start.3 = (f32[4,192]{1,0:T(4,128)S(1)}, f32[4,192]{1,0:T(4,128)S(1)}, u32[]{:S(2)}, u32[]{:S(2)}) collective-permute-start(f32[4,192]{1,0:T(4,128)S(1)} %reshape.138), channel_id=1, source_target_pairs={{0,31},{1,0},{2,1},{3,2},{4,3},{5,4},{6,5},{7,6},{8,7},{9,8},{10,9... | collective-permute-start | bytes 9224 | tf_op jit(solution)/shard_map/ppermute | solution.py:813
  23.7 0.7 copy-start.14
  24.5 0.7 copy-start.15
  31.2 6.9 %copy-start.13 = (f32[32,1]{1,0:T(8,128)S(1)}, f32[32,1]{1,0:T(8,128)}, u32[]{:S(2)}) copy-start(f32[32,1]{1,0:T(8,128)} %get-tuple-element.12) | copy-start | bytes 388
  31.2 15.0 %all-to-all-start.1 = ((f32[32,1,2448]{2,1,0:T(1,128)}), f32[32,1,2448]{2,1,0:T(1,128)S(1)}, u32[]{:S(2)}, u32[]{:S(2)}) async-start(f32[32,1,2448]{2,1,0:T(1,128)} %copy.35), calls=%async_computation.1 | async-start | bytes 655360 | tf_op jit(solution)/shard_map/all_to_all | solution.py:826
  38.3 0.7 copy-start.10
  46.2 0.7 copy-start.8
  46.3 0.9 copy-start
  46.3 0.9 copy-start.2
  46.3 0.9 copy-start.3
  46.3 0.9 copy-start.4
  46.3 0.9 copy-start.5
  46.3 0.9 copy-start.6
  46.3 0.9 copy-start.7
  46.5 0.9 copy-start.1
  46.7 0.8 copy-start.9
  89.3 13.1 %all-to-all-start.2 = ((f32[32,1,2592]{2,1,0:T(1,128)}), f32[32,1,2592]{2,1,0:T(1,128)S(1)}, u32[]{:S(2)}, u32[]{:S(2)}) async-start(f32[32,1,2592]{2,1,0:T(1,128)} %copy.42), calls=%async_computation.2 | async-start | bytes 688128 | tf_op jit(solution)/shard_map/all_to_all | solution.py:862
  102.7 8.6 %collective-permute-start.4 = (f32[3,128]{1,0:T(4,128)S(1)}, f32[3,128]{1,0:T(4,128)S(1)}, u32[]{:S(2)}, u32[]{:S(2)}) collective-permute-start(f32[3,128]{1,0:T(4,128)S(1)} %get-tuple-element.35), channel_id=1, source_target_pairs={{0,32},{32,64},{64,96},{96,0},{1,33},{33,65},{65,97},{97,1},{2,34}... | collective-permute-start | bytes 4616 | tf_op jit(solution)/shard_map/ppermute | solution.py:867
  110.6 4.5 %collective-permute-start.5 = (f32[3,128]{1,0:T(4,128)S(1)}, f32[3,128]{1,0:T(4,128)S(1)}, u32[]{:S(2)}, u32[]{:S(2)}) collective-permute-start(f32[3,128]{1,0:T(4,128)S(1)} %get-tuple-element.36), channel_id=1, source_target_pairs={{0,96},{32,0},{64,32},{96,64},{1,97},{33,1},{65,33},{97,65},{2,98}... | collective-permute-start | bytes 4616 | tf_op jit(solution)/shard_map/ppermute | solution.py:866

commit v3 on v2

--- a/solution.py
+++ b/solution.py
@@ -804,21 +804,32 @@
         [positions.reshape(3, sites), species.reshape(1, sites).astype(F32)], axis=0
     )
     up_x, down_x = ring("gx", 1), ring("gx", -1)
-    up_y, down_y = ring("yz", 1), ring("yz", -1)
     before = lax.ppermute(own[:, 384:512], "gx", up_x)
     after = lax.ppermute(own[:, 0:128], "gx", down_x)
     mid = jnp.concatenate([before, own, after], axis=1)
     planes = mid.reshape(4, 12, 64)
-    low = lax.ppermute(planes[:, :, 48:64].reshape(4, 192), "yz", up_y)
-    high = lax.ppermute(planes[:, :, 0:16].reshape(4, 192), "yz", down_y)
     filled = jnp.max(jnp.where(used > 0, lax.broadcasted_iota(jnp.int32, used.shape, 0) + 1, 0))
     need = (filled + GROUP - 1) // GROUP
 
     last = slice(KEPT * GROUP, sites)
     codes = jnp.where(used[last] > 0, near[last], -1).astype(F32).reshape(3, count, SHARE)
     shares = codes.transpose(1, 0, 2).reshape(count, 3 * SHARE)
-    shares = jnp.concatenate([shares, jnp.full((count, 1), need, jnp.int32).astype(F32)], axis=1)
+    device = jnp.arange(count, dtype=jnp.int32)
+    me_low = (device == (me + count - 1) % count).astype(F32)[:, None]
+    me_high = (device == (me + 1) % count).astype(F32)[:, None]
+    shares = jnp.concatenate(
+        [
+            shares,
+            jnp.full((count, 1), need, jnp.int32).astype(F32),
+            me_high * planes[:, :, 48:64].reshape(1, 768),
+            me_low * planes[:, :, 0:16].reshape(1, 768),
+        ],
+        axis=1,
+    )
     shares = lax.all_to_all(shares, "yz", 0, 0, tiled=True)
+    edges = jnp.sum(shares[:, 3 * SHARE + 1 :], axis=0)
+    low = edges[0:768].reshape(4, 192)
+    high = edges[768:1536].reshape(4, 192)
     box = jnp.concatenate([low.reshape(4, 12, 16), planes, high.reshape(4, 12, 16)], axis=2)
     firsts = [KEPT + LENT * j for j in range(3)]
     boxes = jnp.concatenate([box[:, f // 4 : f // 4 + 6].reshape(1, BOX) for f in firsts], axis=0)
@@ -844,12 +855,9 @@
     def to_high(edge):
         return jnp.pad(edge, ((0, 0), (0, 0), (0, 48))).reshape(1, -1)
 
-    device = jnp.arange(count, dtype=jnp.int32)
     home = lender
     home_low = jnp.roll(lender, -1, axis=0)
     home_high = jnp.roll(lender, 1, axis=0)
-    me_low = (device == (me + count - 1) % count).astype(F32)[:, None]
-    me_high = (device == (me + 1) % count).astype(F32)[:, None]
     sent = (
         home * wide[:, :, 16:80].reshape(1, -1)
         + home_low * to_low(wide[:, :, 0:16])

time: 116 us -> 114 us (0.983)
  starting transfers between devices: 38.1 us -> 26.5 us
  waiting for transfers between devices: 14.5 us -> 23.1 us
    all_to_all x1, waiting for transfers between devices: 0.01 us -> 7.37 us  [on_device(): shares = lax.all_to_all(shares, 'yz', 0, 0, tiled=True)]
    ppermute x2 -> x0, starting transfers between devices: 5.7 us -> none  [the longest x1 4.46 us: on_device(): high = lax.ppermute(planes[:, :, 0:16].reshape(4, 192), 'yz', down_y)]
    ppermute x1, starting transfers between devices: 7.9 us -> 4.27 us  [on_device(): from_before = lax.ppermute(column[:, 640:768], 'gx', up_x)]
    all_to_all x1, starting transfers between devices: 6.89 us -> 4.4 us  [on_device(): lent = lax.all_to_all(forward, 'yz', 0, 0, tiled=True)]
    ppermute x1, waiting for transfers between devices: 0.01 us -> 1.4 us  [on_device(): after = lax.ppermute(own[:, 0:128], 'gx', down_x)]
    unnamed x42 -> x44, local copies, waits for them, and re-layouts: 5.93 us -> 5.58 us
  transfers between devices with their start and end apart: 9 -> 7, of which waited for: 4 -> 6; matrix products, arithmetic and copies ran while one was open for 7% -> 6% of each run, Pallas kernels for 0% -> 0%
where the time goes in v3:
time: 114 us; the launch traced here: 113 us
  Pallas kernels  41.5 us (36%)
  starting transfers between devices  26.5 us (23%)
  waiting for transfers between devices  23.1 us (20%)
  local copies, waits for them, and re-layouts  13.7 us (12%)
  other arithmetic  4.72 us (4%)
  between operations  3.71 us (3%)
    pallas_call x1, Pallas kernels, pair_call(): pl.pallas_call(pair_kernel, out_shape=[jax.ShapeDtypeStruct((sites // GRO...  39.3 us
    all_to_all x1, waiting for transfers between devices, on_device(): lax.all_to_all(jnp.concatenate([sent] + parts, axis=1), 'yz', 0, 0, tiled...  7.99 us
    all_to_all x1, starting transfers between devices, on_device(): shares = lax.all_to_all(shares, 'yz', 0, 0, tiled=True)  7.49 us
    all_to_all x1, waiting for transfers between devices, on_device(): shares = lax.all_to_all(shares, 'yz', 0, 0, tiled=True)  7.37 us
    unnamed x44, local copies, waits for them, and re-layouts  5.58 us
    all_to_all x1, starting transfers between devices, on_device(): lax.all_to_all(jnp.concatenate([sent] + parts, axis=1), 'yz', 0, 0, tiled...  5.26 us
    ppermute x1, starting transfers between devices, on_device(): before = lax.ppermute(own[:, 384:512], 'gx', up_x)  5.06 us
    all_to_all x1, starting transfers between devices, on_device(): lent = lax.all_to_all(forward, 'yz', 0, 0, tiled=True)  4.4 us
  transfers between devices with their start and end apart: 7, of which 6 were waited for; matrix products, arithmetic and copies ran while one was open for 6% of the time, Pallas kernels for 0%

profile of v3, /device:TPU:1, one launch (start us, length us, event | category | flops | bytes accessed | tf_op | source)
XLA Modules:
  0.0 113.3 jit_solution(2430940840187464153)
XLA Ops:
  0.6 0.7 copy.51
  1.4 5.1 %collective-permute-start = (f32[4,128]{1,0:T(4,128)S(1)}, f32[4,128]{1,0:T(4,128)S(1)}, u32[]{:S(2)}, u32[]{:S(2)}) collective-permute-start(f32[4,128]{1,0:T(4,128)S(1)} %get-tuple-element.37), channel_id=1, source_target_pairs={{0,32},{32,64},{64,96},{96,0},{1,33},{33,65},{65,97},{97,1},{2,34}... | collective-permute-start | bytes 6152 | tf_op jit(solution)/shard_map/ppermute | solution.py:807
  6.5 1.1 copy.32
  7.5 0.1 select_convert_fusion
  7.7 0.8 select_reduce_fusion
  9.1 0.1 copy.30
  9.2 0.1 convert_element_type.54
  9.4 0.1 reshape.162
  9.5 1.4 %collective-permute-done.1 = f32[4,128]{1,0:T(4,128)S(1)} collective-permute-done((f32[4,128]{1,0:T(4,128)S(1)}, f32[4,128]{1,0:T(4,128)S(1)}, u32[]{:S(2)}, u32[]{:S(2)}) %collective-permute-start.1) | collective-permute-done | bytes 2080 | tf_op jit(solution)/shard_map/ppermute | solution.py:808
  10.9 0.1 reshape.165
  11.3 0.1 broadcast_multiply_fusion
  11.4 0.1 concatenate.31
  11.5 0.9 all_to_all.21
  12.4 7.5 %all-to-all-start = ((f32[32,1,1969]{2,1,0:T(1,128)}), f32[32,1,1969]{2,1,0:T(1,128)S(1)}, u32[]{:S(2)}, u32[]{:S(2)}) async-start(f32[32,1,1969]{2,1,0:T(1,128)} %all_to_all.21), calls=%async_computation | async-start | bytes 524288 | tf_op jit(solution)/shard_map/all_to_all | solution.py:829
  19.9 0.1 copy.33
  20.1 0.6 copy-done.15
  20.6 0.1 copy.36.env_ref
  20.8 0.6 copy-done.16
  21.3 0.1 copy.35.first_ref
  21.4 7.4 %all-to-all-done = f32[32,1,1969]{2,1,0:T(1,128)S(1)} async-done(((f32[32,1,1969]{2,1,0:T(1,128)}), f32[32,1,1969]{2,1,0:T(1,128)S(1)}, u32[]{:S(2)}, u32[]{:S(2)}) %all-to-all-start) | async-done | bytes 252064 | tf_op jit(solution)/shard_map/all_to_all | solution.py:829
  28.8 0.1 copy.50
  28.9 0.1 slice_reduce_fusion
  29.3 0.1 reshape.170.high_ref
  29.4 0.1 pad_maximum_fusion.1
  29.5 0.1 copy-done.11
  29.6 0.1 reshape.166
  29.7 0.1 reshape.167
  29.8 0.1 reshape.168
  29.9 0.6 pad_maximum_fusion.boxes_ref
  30.5 2.2 %route.1 = (f32[32,2448]{1,0:T(8,128)}, f32[32,1]{1,0:T(8,128)}, s32[4]{0:T(128)}) custom-call(s32[1]{0:T(128)} %bitcast.me_ref, f32[32,1969]{1,0:T(8,128)} %bitcast.40, f32[3,2304]{1,0:T(4,128)} %pad_maximum_fusion.boxes_ref), custom_call_target="tpu_custom_call" | custom-call | tf_op jit(solution)/shard_map/route/pallas_call | solution.py:779
  32.7 2.0 %copy.34 = f32[32,1,2448]{2,1,0:T(1,128)} copy(f32[32,1,2448]{2,0,1:T(8,128)} %bitcast.45) | data formatting | bytes 626688 | tf_op jit(solution)/shard_map/all_to_all | solution.py:837
  34.8 4.4 %all-to-all-start.1 = ((f32[32,1,2448]{2,1,0:T(1,128)}), f32[32,1,2448]{2,1,0:T(1,128)S(1)}, u32[]{:S(2)}, u32[]{:S(2)}) async-start(f32[32,1,2448]{2,1,0:T(1,128)} %copy.34), calls=%async_computation.1 | async-start | bytes 655360 | tf_op jit(solution)/shard_map/all_to_all | solution.py:837
  39.2 0.1 reduce.1
  39.3 0.7 copy-done.10
  40.0 0.6 slice.140
  42.5 0.1 copy.37
  42.6 0.1 copy.40
  42.7 0.6 fusion.6
  43.2 0.7 maximum_bitcast_fusion
  44.0 0.7 maximum_bitcast_fusion.1
  44.7 2.5 %all-to-all-done.1 = f32[32,1,2448]{2,1,0:T(1,128)S(1)} async-done(((f32[32,1,2448]{2,1,0:T(1,128)}), f32[32,1,2448]{2,1,0:T(1,128)S(1)}, u32[]{:S(2)}, u32[]{:S(2)}) %all-to-all-start.1) | async-done | bytes 313376 | tf_op jit(solution)/shard_map/all_to_all | solution.py:837
  47.3 0.2 fusion
  47.5 0.1 reshape.173.lent_sites_ref
  47.5 0.1 reshape.172.lent_ref
  47.6 0.2 copy-done.8
  47.8 0.2 copy-done
  48.2 0.2 copy-done.1
  48.4 39.3 %pair_terms.1 = (f32[40,16]{1,0:T(8,128)S(1)}, f32[3,768]{1,0:T(4,128)S(1)}, f32[3,192]{1,0:T(4,128)S(1)}, f32[3,192]{1,0:T(4,128)S(1)}, f32[3,576]{1,0:T(4,128)S(1)}) custom-call(s32[4]{0:T(128)S(1)} %copy-done.10, f32[4,768]{1,0:T(4,128)S(1)} %pad_maximum_fusion.2.mid_ref, f32[4,192]{1,0:T(4,128)S(1)} %reshape.169.low_ref, ...), custom_call_target="tpu_custom_call" | custom-call | tf_op jit(solution)/shard_map/pair_terms/pallas_call | solution.py:709
  87.7 0.1 reshape.176
  88.0 0.1 mul.179
  88.1 0.1 pad.33
  88.5 0.1 pad.35
  88.8 0.2 multiply_add_fusion
  89.1 0.1 concatenate.36
  89.2 1.1 copy.41
  90.2 5.3 %all-to-all-start.2 = ((f32[32,1,2592]{2,1,0:T(1,128)}), f32[32,1,2592]{2,1,0:T(1,128)S(1)}, u32[]{:S(2)}, u32[]{:S(2)}) async-start(f32[32,1,2592]{2,1,0:T(1,128)} %copy.41), calls=%async_computation.2 | async-start | bytes 688128 | tf_op jit(solution)/shard_map/all_to_all | solution.py:870
  95.6 0.1 reshape.175
  95.6 8.0 %all-to-all-done.2 = f32[32,1,2592]{2,1,0:T(1,128)S(1)} async-done(((f32[32,1,2592]{2,1,0:T(1,128)}), f32[32,1,2592]{2,1,0:T(1,128)S(1)}, u32[]{:S(2)}, u32[]{:S(2)}) %all-to-all-start.2) | async-done | bytes 331808 | tf_op jit(solution)/shard_map/all_to_all | solution.py:870
  103.6 0.2 reduce_sum.29
  103.9 4.3 %collective-permute-start.2 = (f32[3,128]{1,0:T(4,128)S(1)}, f32[3,128]{1,0:T(4,128)S(1)}, u32[]{:S(2)}, u32[]{:S(2)}) collective-permute-start(f32[3,128]{1,0:T(4,128)S(1)} %get-tuple-element.35), channel_id=1, source_target_pairs={{0,32},{32,64},{64,96},{96,0},{1,33},{33,65},{65,97},{97,1},{2,34}... | collective-permute-start | bytes 4616 | tf_op jit(solution)/shard_map/ppermute | solution.py:875
  108.2 0.7 pad_add_fusion
  108.8 0.1 collective-permute-done.2
  108.9 3.8 %collective-permute-done.3 = f32[3,128]{1,0:T(4,128)S(1)} collective-permute-done((f32[3,128]{1,0:T(4,128)S(1)}, f32[3,128]{1,0:T(4,128)S(1)}, u32[]{:S(2)}, u32[]{:S(2)}) %collective-permute-start.3) | collective-permute-done | bytes 1568 | tf_op jit(solution)/shard_map/ppermute | solution.py:874
  112.7 0.6 copy.42
  (73 shorter events, 1.6 us)
Async XLA Ops:
  0.6 0.7 copy-start.17
  1.4 8.2 %collective-permute-start = (f32[4,128]{1,0:T(4,128)S(1)}, f32[4,128]{1,0:T(4,128)S(1)}, u32[]{:S(2)}, u32[]{:S(2)}) collective-permute-start(f32[4,128]{1,0:T(4,128)S(1)} %get-tuple-element.37), channel_id=1, source_target_pairs={{0,32},{32,64},{64,96},{96,0},{1,33},{33,65},{65,97},{97,1},{2,34}... | collective-permute-start | bytes 6152 | tf_op jit(solution)/shard_map/ppermute | solution.py:807
  6.4 4.5 %collective-permute-start.1 = (f32[4,128]{1,0:T(4,128)S(1)}, f32[4,128]{1,0:T(4,128)S(1)}, u32[]{:S(2)}, u32[]{:S(2)}) collective-permute-start(f32[4,128]{1,0:T(4,128)S(1)} %get-tuple-element.38), channel_id=1, source_target_pairs={{0,96},{32,0},{64,32},{96,64},{1,97},{33,1},{65,33},{97,65},{2,98}... | collective-permute-start | bytes 6152 | tf_op jit(solution)/shard_map/ppermute | solution.py:808
  6.4 1.1 copy-start.12
  6.4 1.1 copy-start.13
  12.4 16.4 %all-to-all-start = ((f32[32,1,1969]{2,1,0:T(1,128)}), f32[32,1,1969]{2,1,0:T(1,128)S(1)}, u32[]{:S(2)}, u32[]{:S(2)}) async-start(f32[32,1,1969]{2,1,0:T(1,128)} %all_to_all.21), calls=%async_computation | async-start | bytes 524288 | tf_op jit(solution)/shard_map/all_to_all | solution.py:829
  19.9 0.7 copy-start.15
  20.6 0.7 copy-start.16
  28.9 0.7 copy-start.11
  34.8 4.4 %copy-start.14 = (f32[32,1]{1,0:T(8,128)S(1)}, f32[32,1]{1,0:T(8,128)}, u32[]{:S(2)}) copy-start(f32[32,1]{1,0:T(8,128)} %get-tuple-element.12) | copy-start | bytes 388
  34.8 12.4 %all-to-all-start.1 = ((f32[32,1,2448]{2,1,0:T(1,128)}), f32[32,1,2448]{2,1,0:T(1,128)S(1)}, u32[]{:S(2)}, u32[]{:S(2)}) async-start(f32[32,1,2448]{2,1,0:T(1,128)} %copy.34), calls=%async_computation.1 | async-start | bytes 655360 | tf_op jit(solution)/shard_map/all_to_all | solution.py:837
  39.3 0.7 copy-start.10
  47.2 0.7 copy-start.8
  47.2 0.9 copy-start
  47.2 0.9 copy-start.2
  47.2 0.9 copy-start.3
  47.2 0.9 copy-start.4
  47.2 0.9 copy-start.5
  47.3 0.9 copy-start.6
  47.3 0.9 copy-start.7
  47.4 0.9 copy-start.1
  47.6 0.8 copy-start.9
  90.2 13.4 %all-to-all-start.2 = ((f32[32,1,2592]{2,1,0:T(1,128)}), f32[32,1,2592]{2,1,0:T(1,128)S(1)}, u32[]{:S(2)}, u32[]{:S(2)}) async-start(f32[32,1,2592]{2,1,0:T(1,128)} %copy.41), calls=%async_computation.2 | async-start | bytes 688128 | tf_op jit(solution)/shard_map/all_to_all | solution.py:870
  103.9 5.0 %collective-permute-start.2 = (f32[3,128]{1,0:T(4,128)S(1)}, f32[3,128]{1,0:T(4,128)S(1)}, u32[]{:S(2)}, u32[]{:S(2)}) collective-permute-start(f32[3,128]{1,0:T(4,128)S(1)} %get-tuple-element.35), channel_id=1, source_target_pairs={{0,32},{32,64},{64,96},{96,0},{1,33},{33,65},{65,97},{97,1},{2,34}... | collective-permute-start | bytes 4616 | tf_op jit(solution)/shard_map/ppermute | solution.py:875
  108.2 4.5 %collective-permute-start.3 = (f32[3,128]{1,0:T(4,128)S(1)}, f32[3,128]{1,0:T(4,128)S(1)}, u32[]{:S(2)}, u32[]{:S(2)}) collective-permute-start(f32[3,128]{1,0:T(4,128)S(1)} %get-tuple-element.36), channel_id=1, source_target_pairs={{0,96},{32,0},{64,32},{96,64},{1,97},{33,1},{65,33},{97,65},{2,98}... | collective-permute-start | bytes 4616 | tf_op jit(solution)/shard_map/ppermute | solution.py:874
